TPU v7x, 32 devices: a whole 2x2x4 slice. The times are simulated.
32 devices in a mesh: section: 4 (over y, x), dom: 8 (over z, core).
Axes of the slice: x: 2, y: 2, z: 4, core: 2. Of those that a mesh axis runs over, the one named last changes fastest.
Arguments:
- features: bfloat16 [2, 2048, 128], P(None, 'dom'), may hold values from -6 to 6
- input_weight: bfloat16 [128, 512], replicated, may hold values from -0.5 to 0.5
- layer_weights: bfloat16 [8, 512, 512], P('section'), may hold values from -0.25 to 0.25
- tiles: bfloat16 [2, 16, 4, 128, 128], P(None, 'dom'), may hold values from -0.4375 to 0.4375
- pub_ids: int32 [2, 16], P(None, 'dom'), may hold values from -1 to 1, as said below
- tile_src: int32 [2, 16, 4], P(None, 'dom'), may hold values from 0 to 5, as said below
Outputs:
- section_outputs: bfloat16 [4, 2, 2048, 512], P('section', None, 'dom')
Inputs may be any that keep to these rules, and one draw needn't show every extreme that they name: `pub_ids`: for each node group and partition, its 2 slots hold distinct local block numbers below 2 first and -1 in the unused slots after them; every partition lists at least one block, and in every node group some partition fills all 2 slots. `tile_src`: each entry names a slot of the destination block's partition: a local block below 2, or a listed (not -1) slot of the previous or the next partition; the first partition reads no previous one and the last no next one. In every node group some tile reads the last slot of a next partition.
All inputs are finite; a program needn't handle non-finite values.
Results may differ from a plain program's by a relative error of at most 0.019.
Values may be sent and summed in bfloat16 or wider, within the bound.
No kernel may reach another device: no remote copies, remote signals or barrier semaphores. Data moves between devices by JAX's collectives and lax.ppermute only.
A program may use at most 64 MiB of HBM per device.

v0:
```python
import jax
import jax.numpy as jnp
from jax import lax
from jax.sharding import PartitionSpec as P

residual_share = 0.1
decay_theta = 0.5


def passed_along(block, axis, distance):
    devices = range(lax.axis_size(axis))
    route = [(i - distance, i) for i in devices if i - distance in devices]
    return lax.ppermute(block, axis, route)


def shards(features, input_weight, layer_weights, tiles, pub_ids, tile_src):
    groups = features.shape[0]
    node_rows = features.shape[1]
    block_count = tiles.shape[1]
    tile_count = tiles.shape[2]
    block_rows = tiles.shape[3]
    feature_width = input_weight.shape[1]
    slot_count = pub_ids.shape[1]
    layers_here = layer_weights.shape[0]
    section_index = lax.axis_index("section")
    section_total = lax.axis_size("section")
    total_steps = groups + section_total - 1
    empty_rows = jnp.zeros((node_rows, feature_width), jnp.bfloat16)
    carried_hidden = empty_rows
    collected = jnp.zeros((groups, node_rows, feature_width), jnp.bfloat16)
    for tick in range(total_steps):
        group_index = tick - section_index
        active = (group_index >= 0) & (group_index < groups)
        clamped = jnp.clip(group_index, 0, groups - 1)
        initial = jax.nn.relu(
            jnp.dot(
                lax.dynamic_index_in_dim(features, clamped, 0, keepdims=False),
                input_weight,
                preferred_element_type=jnp.float32,
            )
        ).astype(jnp.bfloat16)
        current = jnp.where(section_index == 0, initial, carried_hidden)
        tile_block = lax.dynamic_index_in_dim(tiles, clamped, 0, keepdims=False)
        sources = lax.dynamic_index_in_dim(tile_src, clamped, 0, keepdims=False)
        listed = lax.dynamic_index_in_dim(pub_ids, clamped, 0, keepdims=False)
        for layer in range(layers_here):
            number = (section_index * layers_here + layer + 1).astype(jnp.float32)
            beta = jnp.log(decay_theta / number + 1.0)
            blocks = current.reshape(block_count, block_rows, feature_width)
            select = (listed[:, None] == jnp.arange(block_count)[None, :]).astype(jnp.bfloat16)
            packed = jnp.einsum("mn,nrd->mrd", select, blocks, preferred_element_type=jnp.float32)
            packed = packed.astype(jnp.bfloat16).reshape(slot_count * block_rows, feature_width)
            received = [passed_along(packed, "dom", offset) for offset in (1, -1)]
            table = jnp.concatenate(
                [blocks] + [piece.reshape(-1, block_rows, feature_width) for piece in received], 0
            )
            gathered = jnp.take(table, sources.reshape(-1), axis=0).reshape(
                block_count, tile_count, block_rows, feature_width
            )
            aggregate = jnp.einsum(
                "bkij,bkjd->bid", tile_block, gathered, preferred_element_type=jnp.float32
            )
            aggregate = aggregate.reshape(node_rows, feature_width)
            support = (
                (1.0 - residual_share) * aggregate + residual_share * initial.astype(jnp.float32)
            ).astype(jnp.bfloat16)
            product = jnp.dot(support, layer_weights[layer], preferred_element_type=jnp.float32)
            mixed = (1.0 - beta) * support.astype(jnp.float32) + beta * product
            current = jax.nn.relu(mixed).astype(jnp.bfloat16)
        previous = lax.dynamic_index_in_dim(collected, clamped, 0, keepdims=False)
        collected = lax.dynamic_update_index_in_dim(
            collected, jnp.where(active, current, previous), clamped, 0
        )
        if tick + 1 < total_steps:
            carried_hidden = passed_along(current, "section", 1)
    return collected[None]


def solution(mesh):
    in_specs = (
        P(None, "dom", None),
        P(),
        P("section", None, None),
        P(None, "dom", None, None, None),
        P(None, "dom"),
        P(None, "dom", None),
    )
    out_specs = P("section", None, "dom", None)
    return jax.shard_map(shards, mesh=mesh, in_specs=in_specs, out_specs=out_specs, check_vma=False)
```

profile of v0, /device:TPU:13, one launch (start us, length us, event | category | flops | bytes accessed | tf_op | source)
XLA Modules:
  0.0 175.3 jit_solution(7879467005975602681)
XLA Ops:
  1.8 3.8 %collective-permute-start = (bf16[256,512]{1,0:T(8,128)(2,1)S(1)}, bf16[256,512]{1,0:T(8,128)(2,1)S(1)}, u32[]{:S(2)}, u32[]{:S(2)}) collective-permute-start(bf16[256,512]{1,0:T(8,128)(2,1)S(1)} %bitcast.323), channel_id=1, source_target_pairs={{0,1},{1,2},{2,3},{3,4},{4,5},{5,6},{6,7},{8,9},{9,10},{10,11},{11... | collective-permute-start | bytes 786440 | tf_op jit(solution)/shard_map/ppermute | solution.py:13
  8.9 4.4 %collective-permute-done.1 = bf16[256,512]{1,0:T(8,128)(2,1)S(1)} collective-permute-done((bf16[256,512]{1,0:T(8,128)(2,1)S(1)}, bf16[256,512]{1,0:T(8,128)(2,1)S(1)}, u32[]{:S(2)}, u32[]{:S(2)}) %collective-permute-start.1) | collective-permute-done | bytes 262176 | tf_op jit(solution)/shard_map/ppermute | solution.py:13
  18.2 2.4 %collective-permute-start.3 = (bf16[256,512]{1,0:T(8,128)(2,1)S(1)}, bf16[256,512]{1,0:T(8,128)(2,1)S(1)}, u32[]{:S(2)}, u32[]{:S(2)}) collective-permute-start(bf16[256,512]{1,0:T(8,128)(2,1)S(1)} %bitcast.326), channel_id=1, source_target_pairs={{1,0},{2,1},{3,2},{4,3},{5,4},{6,5},{7,6},{9,8},{10,9},{11,10},{12... | collective-permute-start | bytes 786440 | tf_op jit(solution)/shard_map/ppermute | solution.py:13
  21.5 4.4 %collective-permute-done.3 = bf16[256,512]{1,0:T(8,128)(2,1)S(1)} collective-permute-done((bf16[256,512]{1,0:T(8,128)(2,1)S(1)}, bf16[256,512]{1,0:T(8,128)(2,1)S(1)}, u32[]{:S(2)}, u32[]{:S(2)}) %collective-permute-start.3) | collective-permute-done | bytes 262176 | tf_op jit(solution)/shard_map/ppermute | solution.py:13
  28.6 3.1 %collective-permute-start.4 = (bf16[256,512]{1,0:T(8,128)(2,1)S(1)}, bf16[256,512]{1,0:T(8,128)(2,1)S(1)}, u32[]{:S(2)}, u32[]{:S(2)}) collective-permute-start(bf16[256,512]{1,0:T(8,128)(2,1)S(1)} %get-tuple-element.19), channel_id=1, source_target_pairs={{0,8},{8,16},{16,24},{1,9},{9,17},{17,25},{2,10},{10,18},{18,26},{... | collective-permute-start | bytes 786440 | tf_op jit(solution)/shard_map/ppermute | solution.py:13
  31.8 6.7 %collective-permute-done.4 = bf16[256,512]{1,0:T(8,128)(2,1)S(1)} collective-permute-done((bf16[256,512]{1,0:T(8,128)(2,1)S(1)}, bf16[256,512]{1,0:T(8,128)(2,1)S(1)}, u32[]{:S(2)}, u32[]{:S(2)}) %collective-permute-start.4) | collective-permute-done | bytes 262176 | tf_op jit(solution)/shard_map/ppermute | solution.py:13
  39.3 2.9 %collective-permute-start.5 = (bf16[256,512]{1,0:T(8,128)(2,1)S(1)}, bf16[256,512]{1,0:T(8,128)(2,1)S(1)}, u32[]{:S(2)}, u32[]{:S(2)}) collective-permute-start(bf16[256,512]{1,0:T(8,128)(2,1)S(1)} %bitcast.331), channel_id=1, source_target_pairs={{0,1},{1,2},{2,3},{3,4},{4,5},{5,6},{6,7},{8,9},{9,10},{10,11},{11... | collective-permute-start | bytes 786440 | tf_op jit(solution)/shard_map/ppermute | solution.py:13
  45.5 4.4 %collective-permute-done.6 = bf16[256,512]{1,0:T(8,128)(2,1)S(1)} collective-permute-done((bf16[256,512]{1,0:T(8,128)(2,1)S(1)}, bf16[256,512]{1,0:T(8,128)(2,1)S(1)}, u32[]{:S(2)}, u32[]{:S(2)}) %collective-permute-start.6) | collective-permute-done | bytes 262176 | tf_op jit(solution)/shard_map/ppermute | solution.py:13
  52.9 1.9 %collective-permute-start.7 = (bf16[256,512]{1,0:T(8,128)(2,1)S(1)}, bf16[256,512]{1,0:T(8,128)(2,1)S(1)}, u32[]{:S(2)}, u32[]{:S(2)}) collective-permute-start(bf16[256,512]{1,0:T(8,128)(2,1)S(1)} %bitcast.333), channel_id=1, source_target_pairs={{0,1},{1,2},{2,3},{3,4},{4,5},{5,6},{6,7},{8,9},{9,10},{10,11},{11... | collective-permute-start | bytes 786440 | tf_op jit(solution)/shard_map/ppermute | solution.py:13
  54.8 2.4 %collective-permute-start.8 = (bf16[256,512]{1,0:T(8,128)(2,1)S(1)}, bf16[256,512]{1,0:T(8,128)(2,1)S(1)}, u32[]{:S(2)}, u32[]{:S(2)}) collective-permute-start(bf16[256,512]{1,0:T(8,128)(2,1)S(1)} %bitcast.334), channel_id=1, source_target_pairs={{1,0},{2,1},{3,2},{4,3},{5,4},{6,5},{7,6},{9,8},{10,9},{11,10},{12... | collective-permute-start | bytes 786440 | tf_op jit(solution)/shard_map/ppermute | solution.py:13
  58.1 4.4 %collective-permute-done.8 = bf16[256,512]{1,0:T(8,128)(2,1)S(1)} collective-permute-done((bf16[256,512]{1,0:T(8,128)(2,1)S(1)}, bf16[256,512]{1,0:T(8,128)(2,1)S(1)}, u32[]{:S(2)}, u32[]{:S(2)}) %collective-permute-start.8) | collective-permute-done | bytes 262176 | tf_op jit(solution)/shard_map/ppermute | solution.py:13
  65.1 2.2 %collective-permute-start.9 = (bf16[256,512]{1,0:T(8,128)(2,1)S(1)}, bf16[256,512]{1,0:T(8,128)(2,1)S(1)}, u32[]{:S(2)}, u32[]{:S(2)}) collective-permute-start(bf16[256,512]{1,0:T(8,128)(2,1)S(1)} %get-tuple-element.23), channel_id=1, source_target_pairs={{0,8},{8,16},{16,24},{1,9},{9,17},{17,25},{2,10},{10,18},{18,26},{... | collective-permute-start | bytes 786440 | tf_op jit(solution)/shard_map/ppermute | solution.py:13
  67.3 7.7 %collective-permute-done.9 = bf16[256,512]{1,0:T(8,128)(2,1)S(1)} collective-permute-done((bf16[256,512]{1,0:T(8,128)(2,1)S(1)}, bf16[256,512]{1,0:T(8,128)(2,1)S(1)}, u32[]{:S(2)}, u32[]{:S(2)}) %collective-permute-start.9) | collective-permute-done | bytes 262176 | tf_op jit(solution)/shard_map/ppermute | solution.py:13
  75.8 3.7 %collective-permute-start.10 = (bf16[256,512]{1,0:T(8,128)(2,1)S(1)}, bf16[256,512]{1,0:T(8,128)(2,1)S(1)}, u32[]{:S(2)}, u32[]{:S(2)}) collective-permute-start(bf16[256,512]{1,0:T(8,128)(2,1)S(1)} %bitcast.339), channel_id=1, source_target_pairs={{0,1},{1,2},{2,3},{3,4},{4,5},{5,6},{6,7},{8,9},{9,10},{10,11},{11... | collective-permute-start | bytes 786440 | tf_op jit(solution)/shard_map/ppermute | solution.py:13
  82.8 4.4 %collective-permute-done.11 = bf16[256,512]{1,0:T(8,128)(2,1)S(1)} collective-permute-done((bf16[256,512]{1,0:T(8,128)(2,1)S(1)}, bf16[256,512]{1,0:T(8,128)(2,1)S(1)}, u32[]{:S(2)}, u32[]{:S(2)}) %collective-permute-start.11) | collective-permute-done | bytes 262176 | tf_op jit(solution)/shard_map/ppermute | solution.py:13
  90.1 1.9 %collective-permute-start.12 = (bf16[256,512]{1,0:T(8,128)(2,1)S(1)}, bf16[256,512]{1,0:T(8,128)(2,1)S(1)}, u32[]{:S(2)}, u32[]{:S(2)}) collective-permute-start(bf16[256,512]{1,0:T(8,128)(2,1)S(1)} %bitcast.335), channel_id=1, source_target_pairs={{0,1},{1,2},{2,3},{3,4},{4,5},{5,6},{6,7},{8,9},{9,10},{10,11},{11... | collective-permute-start | bytes 786440 | tf_op jit(solution)/shard_map/ppermute | solution.py:13
  92.0 2.4 %collective-permute-start.13 = (bf16[256,512]{1,0:T(8,128)(2,1)S(1)}, bf16[256,512]{1,0:T(8,128)(2,1)S(1)}, u32[]{:S(2)}, u32[]{:S(2)}) collective-permute-start(bf16[256,512]{1,0:T(8,128)(2,1)S(1)} %bitcast.336), channel_id=1, source_target_pairs={{1,0},{2,1},{3,2},{4,3},{5,4},{6,5},{7,6},{9,8},{10,9},{11,10},{12... | collective-permute-start | bytes 786440 | tf_op jit(solution)/shard_map/ppermute | solution.py:13
  95.3 4.4 %collective-permute-done.13 = bf16[256,512]{1,0:T(8,128)(2,1)S(1)} collective-permute-done((bf16[256,512]{1,0:T(8,128)(2,1)S(1)}, bf16[256,512]{1,0:T(8,128)(2,1)S(1)}, u32[]{:S(2)}, u32[]{:S(2)}) %collective-permute-start.13) | collective-permute-done | bytes 262176 | tf_op jit(solution)/shard_map/ppermute | solution.py:13
  104.4 7.9 %collective-permute-done.14 = bf16[256,512]{1,0:T(8,128)(2,1)S(1)} collective-permute-done((bf16[256,512]{1,0:T(8,128)(2,1)S(1)}, bf16[256,512]{1,0:T(8,128)(2,1)S(1)}, u32[]{:S(2)}, u32[]{:S(2)}) %collective-permute-start.14) | collective-permute-done | bytes 262176 | tf_op jit(solution)/shard_map/ppermute | solution.py:13
  113.0 3.0 %collective-permute-start.15 = (bf16[256,512]{1,0:T(8,128)(2,1)S(1)}, bf16[256,512]{1,0:T(8,128)(2,1)S(1)}, u32[]{:S(2)}, u32[]{:S(2)}) collective-permute-start(bf16[256,512]{1,0:T(8,128)(2,1)S(1)} %bitcast.329), channel_id=1, source_target_pairs={{0,1},{1,2},{2,3},{3,4},{4,5},{5,6},{6,7},{8,9},{9,10},{10,11},{11... | collective-permute-start | bytes 786440 | tf_op jit(solution)/shard_map/ppermute | solution.py:13
  116.0 1.9 %collective-permute-start.16 = (bf16[256,512]{1,0:T(8,128)(2,1)S(1)}, bf16[256,512]{1,0:T(8,128)(2,1)S(1)}, u32[]{:S(2)}, u32[]{:S(2)}) collective-permute-start(bf16[256,512]{1,0:T(8,128)(2,1)S(1)} %bitcast.330), channel_id=1, source_target_pairs={{1,0},{2,1},{3,2},{4,3},{5,4},{6,5},{7,6},{9,8},{10,9},{11,10},{12... | collective-permute-start | bytes 786440 | tf_op jit(solution)/shard_map/ppermute | solution.py:13
  119.3 4.4 %collective-permute-done.16 = bf16[256,512]{1,0:T(8,128)(2,1)S(1)} collective-permute-done((bf16[256,512]{1,0:T(8,128)(2,1)S(1)}, bf16[256,512]{1,0:T(8,128)(2,1)S(1)}, u32[]{:S(2)}, u32[]{:S(2)}) %collective-permute-start.16) | collective-permute-done | bytes 262176 | tf_op jit(solution)/shard_map/ppermute | solution.py:13
  126.7 1.9 %collective-permute-start.17 = (bf16[256,512]{1,0:T(8,128)(2,1)S(1)}, bf16[256,512]{1,0:T(8,128)(2,1)S(1)}, u32[]{:S(2)}, u32[]{:S(2)}) collective-permute-start(bf16[256,512]{1,0:T(8,128)(2,1)S(1)} %bitcast.337), channel_id=1, source_target_pairs={{0,1},{1,2},{2,3},{3,4},{4,5},{5,6},{6,7},{8,9},{9,10},{10,11},{11... | collective-permute-start | bytes 786440 | tf_op jit(solution)/shard_map/ppermute | solution.py:13
  128.6 2.6 %collective-permute-start.18 = (bf16[256,512]{1,0:T(8,128)(2,1)S(1)}, bf16[256,512]{1,0:T(8,128)(2,1)S(1)}, u32[]{:S(2)}, u32[]{:S(2)}) collective-permute-start(bf16[256,512]{1,0:T(8,128)(2,1)S(1)} %bitcast.338), channel_id=1, source_target_pairs={{1,0},{2,1},{3,2},{4,3},{5,4},{6,5},{7,6},{9,8},{10,9},{11,10},{12... | collective-permute-start | bytes 786440 | tf_op jit(solution)/shard_map/ppermute | solution.py:13
  131.9 4.4 %collective-permute-done.18 = bf16[256,512]{1,0:T(8,128)(2,1)S(1)} collective-permute-done((bf16[256,512]{1,0:T(8,128)(2,1)S(1)}, bf16[256,512]{1,0:T(8,128)(2,1)S(1)}, u32[]{:S(2)}, u32[]{:S(2)}) %collective-permute-start.18) | collective-permute-done | bytes 262176 | tf_op jit(solution)/shard_map/ppermute | solution.py:13
  138.9 1.9 %collective-permute-start.19 = (bf16[256,512]{1,0:T(8,128)(2,1)S(1)}, bf16[256,512]{1,0:T(8,128)(2,1)S(1)}, u32[]{:S(2)}, u32[]{:S(2)}) collective-permute-start(bf16[256,512]{1,0:T(8,128)(2,1)S(1)} %get-tuple-element.31), channel_id=1, source_target_pairs={{0,8},{8,16},{16,24},{1,9},{9,17},{17,25},{2,10},{10,18},{18,26},{... | collective-permute-start | bytes 786440 | tf_op jit(solution)/shard_map/ppermute | solution.py:13
  140.8 8.0 %collective-permute-done.19 = bf16[256,512]{1,0:T(8,128)(2,1)S(1)} collective-permute-done((bf16[256,512]{1,0:T(8,128)(2,1)S(1)}, bf16[256,512]{1,0:T(8,128)(2,1)S(1)}, u32[]{:S(2)}, u32[]{:S(2)}) %collective-permute-start.19) | collective-permute-done | bytes 262176 | tf_op jit(solution)/shard_map/ppermute | solution.py:13
  149.5 2.4 %collective-permute-start.20 = (bf16[256,512]{1,0:T(8,128)(2,1)S(1)}, bf16[256,512]{1,0:T(8,128)(2,1)S(1)}, u32[]{:S(2)}, u32[]{:S(2)}) collective-permute-start(bf16[256,512]{1,0:T(8,128)(2,1)S(1)} %bitcast.341), channel_id=1, source_target_pairs={{0,1},{1,2},{2,3},{3,4},{4,5},{5,6},{6,7},{8,9},{9,10},{10,11},{11... | collective-permute-start | bytes 786440 | tf_op jit(solution)/shard_map/ppermute | solution.py:13
  151.9 2.0 %collective-permute-start.21 = (bf16[256,512]{1,0:T(8,128)(2,1)S(1)}, bf16[256,512]{1,0:T(8,128)(2,1)S(1)}, u32[]{:S(2)}, u32[]{:S(2)}) collective-permute-start(bf16[256,512]{1,0:T(8,128)(2,1)S(1)} %bitcast.342), channel_id=1, source_target_pairs={{1,0},{2,1},{3,2},{4,3},{5,4},{6,5},{7,6},{9,8},{10,9},{11,10},{12... | collective-permute-start | bytes 786440 | tf_op jit(solution)/shard_map/ppermute | solution.py:13
  155.2 4.4 %collective-permute-done.21 = bf16[256,512]{1,0:T(8,128)(2,1)S(1)} collective-permute-done((bf16[256,512]{1,0:T(8,128)(2,1)S(1)}, bf16[256,512]{1,0:T(8,128)(2,1)S(1)}, u32[]{:S(2)}, u32[]{:S(2)}) %collective-permute-start.21) | collective-permute-done | bytes 262176 | tf_op jit(solution)/shard_map/ppermute | solution.py:13
  164.5 2.4 %collective-permute-start.23 = (bf16[256,512]{1,0:T(8,128)(2,1)S(1)}, bf16[256,512]{1,0:T(8,128)(2,1)S(1)}, u32[]{:S(2)}, u32[]{:S(2)}) collective-permute-start(bf16[256,512]{1,0:T(8,128)(2,1)S(1)} %bitcast.328), channel_id=1, source_target_pairs={{1,0},{2,1},{3,2},{4,3},{5,4},{6,5},{7,6},{9,8},{10,9},{11,10},{12... | collective-permute-start | bytes 786440 | tf_op jit(solution)/shard_map/ppermute | solution.py:13
  167.8 4.4 %collective-permute-done.23 = bf16[256,512]{1,0:T(8,128)(2,1)S(1)} collective-permute-done((bf16[256,512]{1,0:T(8,128)(2,1)S(1)}, bf16[256,512]{1,0:T(8,128)(2,1)S(1)}, u32[]{:S(2)}, u32[]{:S(2)}) %collective-permute-start.23) | collective-permute-done | bytes 262176 | tf_op jit(solution)/shard_map/ppermute | solution.py:13
  (162 shorter events, 55.0 us)
Async XLA Ops:
  0.0 14.2 %copy-start = (bf16[2,2,4,128,128]{4,3,2,1,0:T(8,128)(2,1)S(1)}, bf16[2,2,4,128,128]{4,3,2,1,0:T(8,128)(2,1)}, u32[]{:S(2)}) copy-start(bf16[2,2,4,128,128]{4,3,2,1,0:T(8,128)(2,1)} %param.11) | copy-start | bytes 1572868
  0.0 1.2 copy-start.7
  1.8 5.8 %copy-start.6 = (s32[2,2,4]{2,1,0:T(2,128)S(1)}, s32[2,2,4]{2,1,0:T(2,128)}, u32[]{:S(2)}) copy-start(s32[2,2,4]{2,1,0:T(2,128)} %param.13) | copy-start | bytes 196
  1.8 7.1 %collective-permute-start = (bf16[256,512]{1,0:T(8,128)(2,1)S(1)}, bf16[256,512]{1,0:T(8,128)(2,1)S(1)}, u32[]{:S(2)}, u32[]{:S(2)}) collective-permute-start(bf16[256,512]{1,0:T(8,128)(2,1)S(1)} %bitcast.323), channel_id=1, source_target_pairs={{0,1},{1,2},{2,3},{3,4},{4,5},{5,6},{6,7},{8,9},{9,10},{10,11},{11... | collective-permute-start | bytes 786440 | tf_op jit(solution)/shard_map/ppermute | solution.py:13
  5.6 7.7 %collective-permute-start.1 = (bf16[256,512]{1,0:T(8,128)(2,1)S(1)}, bf16[256,512]{1,0:T(8,128)(2,1)S(1)}, u32[]{:S(2)}, u32[]{:S(2)}) collective-permute-start(bf16[256,512]{1,0:T(8,128)(2,1)S(1)} %bitcast.324), channel_id=1, source_target_pairs={{1,0},{2,1},{3,2},{4,3},{5,4},{6,5},{7,6},{9,8},{10,9},{11,10},{12... | collective-permute-start | bytes 786440 | tf_op jit(solution)/shard_map/ppermute | solution.py:13
  16.2 5.2 %collective-permute-start.2 = (bf16[256,512]{1,0:T(8,128)(2,1)S(1)}, bf16[256,512]{1,0:T(8,128)(2,1)S(1)}, u32[]{:S(2)}, u32[]{:S(2)}) collective-permute-start(bf16[256,512]{1,0:T(8,128)(2,1)S(1)} %bitcast.325), channel_id=1, source_target_pairs={{0,1},{1,2},{2,3},{3,4},{4,5},{5,6},{6,7},{8,9},{9,10},{10,11},{11... | collective-permute-start | bytes 786440 | tf_op jit(solution)/shard_map/ppermute | solution.py:13
  18.2 7.7 %collective-permute-start.3 = (bf16[256,512]{1,0:T(8,128)(2,1)S(1)}, bf16[256,512]{1,0:T(8,128)(2,1)S(1)}, u32[]{:S(2)}, u32[]{:S(2)}) collective-permute-start(bf16[256,512]{1,0:T(8,128)(2,1)S(1)} %bitcast.326), channel_id=1, source_target_pairs={{1,0},{2,1},{3,2},{4,3},{5,4},{6,5},{7,6},{9,8},{10,9},{11,10},{12... | collective-permute-start | bytes 786440 | tf_op jit(solution)/shard_map/ppermute | solution.py:13
  28.3 10.3 %copy-start.1 = (bf16[128,512]{1,0:T(8,128)(2,1)S(1)}, bf16[128,512]{1,0:T(8,128)(2,1)}, u32[]{:S(2)}) copy-start(bf16[128,512]{1,0:T(8,128)(2,1)} %param.9) | copy-start | bytes 393220
  28.3 10.3 %copy-start.2 = (bf16[2,256,128]{2,1,0:T(8,128)(2,1)S(1)}, bf16[2,256,128]{2,1,0:T(8,128)(2,1)}, u32[]{:S(2)}) copy-start(bf16[2,256,128]{2,1,0:T(8,128)(2,1)} %param.8) | copy-start | bytes 393220
  28.6 9.9 %collective-permute-start.4 = (bf16[256,512]{1,0:T(8,128)(2,1)S(1)}, bf16[256,512]{1,0:T(8,128)(2,1)S(1)}, u32[]{:S(2)}, u32[]{:S(2)}) collective-permute-start(bf16[256,512]{1,0:T(8,128)(2,1)S(1)} %get-tuple-element.19), channel_id=1, source_target_pairs={{0,8},{8,16},{16,24},{1,9},{9,17},{17,25},{2,10},{10,18},{18,26},{... | collective-permute-start | bytes 786440 | tf_op jit(solution)/shard_map/ppermute | solution.py:13
  39.3 6.2 %collective-permute-start.5 = (bf16[256,512]{1,0:T(8,128)(2,1)S(1)}, bf16[256,512]{1,0:T(8,128)(2,1)S(1)}, u32[]{:S(2)}, u32[]{:S(2)}) collective-permute-start(bf16[256,512]{1,0:T(8,128)(2,1)S(1)} %bitcast.331), channel_id=1, source_target_pairs={{0,1},{1,2},{2,3},{3,4},{4,5},{5,6},{6,7},{8,9},{9,10},{10,11},{11... | collective-permute-start | bytes 786440 | tf_op jit(solution)/shard_map/ppermute | solution.py:13
  42.3 7.7 %collective-permute-start.6 = (bf16[256,512]{1,0:T(8,128)(2,1)S(1)}, bf16[256,512]{1,0:T(8,128)(2,1)S(1)}, u32[]{:S(2)}, u32[]{:S(2)}) collective-permute-start(bf16[256,512]{1,0:T(8,128)(2,1)S(1)} %bitcast.332), channel_id=1, source_target_pairs={{1,0},{2,1},{3,2},{4,3},{5,4},{6,5},{7,6},{9,8},{10,9},{11,10},{12... | collective-permute-start | bytes 786440 | tf_op jit(solution)/shard_map/ppermute | solution.py:13
  50.8 1.2 copy-start.10
  52.9 5.2 %collective-permute-start.7 = (bf16[256,512]{1,0:T(8,128)(2,1)S(1)}, bf16[256,512]{1,0:T(8,128)(2,1)S(1)}, u32[]{:S(2)}, u32[]{:S(2)}) collective-permute-start(bf16[256,512]{1,0:T(8,128)(2,1)S(1)} %bitcast.333), channel_id=1, source_target_pairs={{0,1},{1,2},{2,3},{3,4},{4,5},{5,6},{6,7},{8,9},{9,10},{10,11},{11... | collective-permute-start | bytes 786440 | tf_op jit(solution)/shard_map/ppermute | solution.py:13
  54.8 7.7 %collective-permute-start.8 = (bf16[256,512]{1,0:T(8,128)(2,1)S(1)}, bf16[256,512]{1,0:T(8,128)(2,1)S(1)}, u32[]{:S(2)}, u32[]{:S(2)}) collective-permute-start(bf16[256,512]{1,0:T(8,128)(2,1)S(1)} %bitcast.334), channel_id=1, source_target_pairs={{1,0},{2,1},{3,2},{4,3},{5,4},{6,5},{7,6},{9,8},{10,9},{11,10},{12... | collective-permute-start | bytes 786440 | tf_op jit(solution)/shard_map/ppermute | solution.py:13
  63.4 1.2 copy-start.11
  65.1 9.9 %collective-permute-start.9 = (bf16[256,512]{1,0:T(8,128)(2,1)S(1)}, bf16[256,512]{1,0:T(8,128)(2,1)S(1)}, u32[]{:S(2)}, u32[]{:S(2)}) collective-permute-start(bf16[256,512]{1,0:T(8,128)(2,1)S(1)} %get-tuple-element.23), channel_id=1, source_target_pairs={{0,8},{8,16},{16,24},{1,9},{9,17},{17,25},{2,10},{10,18},{18,26},{... | collective-permute-start | bytes 786440 | tf_op jit(solution)/shard_map/ppermute | solution.py:13
  75.8 7.0 %collective-permute-start.10 = (bf16[256,512]{1,0:T(8,128)(2,1)S(1)}, bf16[256,512]{1,0:T(8,128)(2,1)S(1)}, u32[]{:S(2)}, u32[]{:S(2)}) collective-permute-start(bf16[256,512]{1,0:T(8,128)(2,1)S(1)} %bitcast.339), channel_id=1, source_target_pairs={{0,1},{1,2},{2,3},{3,4},{4,5},{5,6},{6,7},{8,9},{9,10},{10,11},{11... | collective-permute-start | bytes 786440 | tf_op jit(solution)/shard_map/ppermute | solution.py:13
  79.5 7.7 %collective-permute-start.11 = (bf16[256,512]{1,0:T(8,128)(2,1)S(1)}, bf16[256,512]{1,0:T(8,128)(2,1)S(1)}, u32[]{:S(2)}, u32[]{:S(2)}) collective-permute-start(bf16[256,512]{1,0:T(8,128)(2,1)S(1)} %bitcast.340), channel_id=1, source_target_pairs={{1,0},{2,1},{3,2},{4,3},{5,4},{6,5},{7,6},{9,8},{10,9},{11,10},{12... | collective-permute-start | bytes 786440 | tf_op jit(solution)/shard_map/ppermute | solution.py:13
  88.1 1.2 copy-start.12
  90.1 5.2 %collective-permute-start.12 = (bf16[256,512]{1,0:T(8,128)(2,1)S(1)}, bf16[256,512]{1,0:T(8,128)(2,1)S(1)}, u32[]{:S(2)}, u32[]{:S(2)}) collective-permute-start(bf16[256,512]{1,0:T(8,128)(2,1)S(1)} %bitcast.335), channel_id=1, source_target_pairs={{0,1},{1,2},{2,3},{3,4},{4,5},{5,6},{6,7},{8,9},{9,10},{10,11},{11... | collective-permute-start | bytes 786440 | tf_op jit(solution)/shard_map/ppermute | solution.py:13
  92.0 7.7 %collective-permute-start.13 = (bf16[256,512]{1,0:T(8,128)(2,1)S(1)}, bf16[256,512]{1,0:T(8,128)(2,1)S(1)}, u32[]{:S(2)}, u32[]{:S(2)}) collective-permute-start(bf16[256,512]{1,0:T(8,128)(2,1)S(1)} %bitcast.336), channel_id=1, source_target_pairs={{1,0},{2,1},{3,2},{4,3},{5,4},{6,5},{7,6},{9,8},{10,9},{11,10},{12... | collective-permute-start | bytes 786440 | tf_op jit(solution)/shard_map/ppermute | solution.py:13
  102.3 9.9 %collective-permute-start.14 = (bf16[256,512]{1,0:T(8,128)(2,1)S(1)}, bf16[256,512]{1,0:T(8,128)(2,1)S(1)}, u32[]{:S(2)}, u32[]{:S(2)}) collective-permute-start(bf16[256,512]{1,0:T(8,128)(2,1)S(1)} %get-tuple-element.27), channel_id=1, source_target_pairs={{0,8},{8,16},{16,24},{1,9},{9,17},{17,25},{2,10},{10,18},{18,26},{... | collective-permute-start | bytes 786440 | tf_op jit(solution)/shard_map/ppermute | solution.py:13
  113.0 6.3 %collective-permute-start.15 = (bf16[256,512]{1,0:T(8,128)(2,1)S(1)}, bf16[256,512]{1,0:T(8,128)(2,1)S(1)}, u32[]{:S(2)}, u32[]{:S(2)}) collective-permute-start(bf16[256,512]{1,0:T(8,128)(2,1)S(1)} %bitcast.329), channel_id=1, source_target_pairs={{0,1},{1,2},{2,3},{3,4},{4,5},{5,6},{6,7},{8,9},{9,10},{10,11},{11... | collective-permute-start | bytes 786440 | tf_op jit(solution)/shard_map/ppermute | solution.py:13
  116.0 7.7 %collective-permute-start.16 = (bf16[256,512]{1,0:T(8,128)(2,1)S(1)}, bf16[256,512]{1,0:T(8,128)(2,1)S(1)}, u32[]{:S(2)}, u32[]{:S(2)}) collective-permute-start(bf16[256,512]{1,0:T(8,128)(2,1)S(1)} %bitcast.330), channel_id=1, source_target_pairs={{1,0},{2,1},{3,2},{4,3},{5,4},{6,5},{7,6},{9,8},{10,9},{11,10},{12... | collective-permute-start | bytes 786440 | tf_op jit(solution)/shard_map/ppermute | solution.py:13
  126.7 5.3 %collective-permute-start.17 = (bf16[256,512]{1,0:T(8,128)(2,1)S(1)}, bf16[256,512]{1,0:T(8,128)(2,1)S(1)}, u32[]{:S(2)}, u32[]{:S(2)}) collective-permute-start(bf16[256,512]{1,0:T(8,128)(2,1)S(1)} %bitcast.337), channel_id=1, source_target_pairs={{0,1},{1,2},{2,3},{3,4},{4,5},{5,6},{6,7},{8,9},{9,10},{10,11},{11... | collective-permute-start | bytes 786440 | tf_op jit(solution)/shard_map/ppermute | solution.py:13
  128.6 7.7 %collective-permute-start.18 = (bf16[256,512]{1,0:T(8,128)(2,1)S(1)}, bf16[256,512]{1,0:T(8,128)(2,1)S(1)}, u32[]{:S(2)}, u32[]{:S(2)}) collective-permute-start(bf16[256,512]{1,0:T(8,128)(2,1)S(1)} %bitcast.338), channel_id=1, source_target_pairs={{1,0},{2,1},{3,2},{4,3},{5,4},{6,5},{7,6},{9,8},{10,9},{11,10},{12... | collective-permute-start | bytes 786440 | tf_op jit(solution)/shard_map/ppermute | solution.py:13
  138.9 9.9 %collective-permute-start.19 = (bf16[256,512]{1,0:T(8,128)(2,1)S(1)}, bf16[256,512]{1,0:T(8,128)(2,1)S(1)}, u32[]{:S(2)}, u32[]{:S(2)}) collective-permute-start(bf16[256,512]{1,0:T(8,128)(2,1)S(1)} %get-tuple-element.31), channel_id=1, source_target_pairs={{0,8},{8,16},{16,24},{1,9},{9,17},{17,25},{2,10},{10,18},{18,26},{... | collective-permute-start | bytes 786440 | tf_op jit(solution)/shard_map/ppermute | solution.py:13
  149.5 5.7 %collective-permute-start.20 = (bf16[256,512]{1,0:T(8,128)(2,1)S(1)}, bf16[256,512]{1,0:T(8,128)(2,1)S(1)}, u32[]{:S(2)}, u32[]{:S(2)}) collective-permute-start(bf16[256,512]{1,0:T(8,128)(2,1)S(1)} %bitcast.341), channel_id=1, source_target_pairs={{0,1},{1,2},{2,3},{3,4},{4,5},{5,6},{6,7},{8,9},{9,10},{10,11},{11... | collective-permute-start | bytes 786440 | tf_op jit(solution)/shard_map/ppermute | solution.py:13
  151.9 7.7 %collective-permute-start.21 = (bf16[256,512]{1,0:T(8,128)(2,1)S(1)}, bf16[256,512]{1,0:T(8,128)(2,1)S(1)}, u32[]{:S(2)}, u32[]{:S(2)}) collective-permute-start(bf16[256,512]{1,0:T(8,128)(2,1)S(1)} %bitcast.342), channel_id=1, source_target_pairs={{1,0},{2,1},{3,2},{4,3},{5,4},{6,5},{7,6},{9,8},{10,9},{11,10},{12... | collective-permute-start | bytes 786440 | tf_op jit(solution)/shard_map/ppermute | solution.py:13
  162.5 5.2 %collective-permute-start.22 = (bf16[256,512]{1,0:T(8,128)(2,1)S(1)}, bf16[256,512]{1,0:T(8,128)(2,1)S(1)}, u32[]{:S(2)}, u32[]{:S(2)}) collective-permute-start(bf16[256,512]{1,0:T(8,128)(2,1)S(1)} %bitcast.327), channel_id=1, source_target_pairs={{0,1},{1,2},{2,3},{3,4},{4,5},{5,6},{6,7},{8,9},{9,10},{10,11},{11... | collective-permute-start | bytes 786440 | tf_op jit(solution)/shard_map/ppermute | solution.py:13
  164.5 7.7 %collective-permute-start.23 = (bf16[256,512]{1,0:T(8,128)(2,1)S(1)}, bf16[256,512]{1,0:T(8,128)(2,1)S(1)}, u32[]{:S(2)}, u32[]{:S(2)}) collective-permute-start(bf16[256,512]{1,0:T(8,128)(2,1)S(1)} %bitcast.328), channel_id=1, source_target_pairs={{1,0},{2,1},{3,2},{4,3},{5,4},{6,5},{7,6},{9,8},{10,9},{11,10},{12... | collective-permute-start | bytes 786440 | tf_op jit(solution)/shard_map/ppermute | solution.py:13
  (10 other events, 11.7 us)
where the time goes:
time: 177 us; the launch traced here: 175 us
  waiting for transfers between devices  81.6 us (46%)
  starting transfers between devices  56.4 us (32%)
  local copies, waits for them, and re-layouts  18.8 us (11%)
  matrix products  13.9 us (8%)
  other arithmetic  3.34 us (2%)
    ppermute x24, waiting for transfers between devices, passed_along(): return lax.ppermute(block, axis, route)  81.6 us
    ppermute x24, starting transfers between devices, passed_along(): return lax.ppermute(block, axis, route)  56.4 us
    unnamed x37, local copies, waits for them, and re-layouts  9.67 us
    gather x10, local copies, waits for them, and re-layouts, shards(): jnp.take(table, sources.reshape(-1), axis=0)  6.14 us
    dot_general x10, matrix products, shards(): jnp.einsum('mn,nrd->mrd', select, blocks, preferred_element_type=jnp.floa...  4.86 us
    dot_general x10, matrix products, shards(): jnp.dot(support, layer_weights[layer], preferred_element_type=jnp.float32)  3.93 us
  transfers between devices with their start and end apart: 24, of which 23 were waited for; matrix products, arithmetic and copies ran while one was open for 2% of the time, Pallas kernels for 0%

commit v1 on v0

v1 whole, which is shorter than its diff:
```python
import functools
import math

import jax
import jax.numpy as jnp
from jax import lax
from jax.experimental import pallas as pl
from jax.experimental.pallas import tpu as pltpu
from jax.sharding import PartitionSpec as P

residual_share = 0.1
decay_theta = 0.5
vmem_bytes = 44 * 2**20
meta_rows = 32


def swapped(block, axis, mask):
    return lax.ppermute(block, axis, [(i, i ^ mask) for i in range(lax.axis_size(axis))])


def shifted(block, axis, distance):
    devices = range(lax.axis_size(axis))
    return lax.ppermute(block, axis, [(i + distance, i) for i in devices if i + distance in devices])


def one_way(block, axis, pairs):
    return lax.ppermute(block, axis, pairs)


def cone_kernel(dims, *refs):
    (parts, in_order, layers, per_section, blocks, tile_count, listed_count, tile_rows, rows, slots, shares) = dims
    place_ref, entry_ref = refs[:2]
    pieces = refs[2 : 2 + parts]
    inputs = refs[2 + parts : 2 + parts + len(shares)]
    placed_ref, sent_ref = refs[2 + parts + len(shares) : 4 + parts + len(shares)]
    layer_weight, band, initial, even, odd, notes, plan, sems, plan_sem = refs[4 + parts + len(shares) :]
    own, section, core, group = [place_ref[i] for i in range(4)]
    states = (even, odd)
    tile_area = blocks * tile_count * tile_rows

    def copy(index):
        mask, flip = shares[index]
        target = layer_weight.at[pl.ds((section ^ mask) * per_section, per_section)]
        if flip is not None:
            size = inputs[index].shape[1]
            target = target.at[:, pl.ds(pl.multiple_of((core ^ flip) * size, size), size)]
        return pltpu.make_async_copy(inputs[index], target, sems.at[index])

    for index in range(len(inputs)):
        copy(index).start()
    for slot in range(parts):
        line = pieces[slot][tile_area + rows :].astype(jnp.float32)
        notes[slot : slot + 1] = line[0:1].astype(jnp.int32)
    to_scalars = pltpu.make_async_copy(notes, plan, plan_sem)
    to_scalars.start()
    empty = jnp.zeros((rows, even.shape[1]), jnp.bfloat16)
    for state in states:
        state[0:rows] = empty
        state[(parts + 1) * rows : (parts + 2) * rows] = empty

    def slot_of(position):
        return position if in_order else position ^ own

    for slot in range(parts):
        position = slot_of(slots[slot])
        value = jnp.dot(pieces[slot][tile_area : tile_area + rows], entry_ref[...], preferred_element_type=jnp.float32)
        value = jnp.maximum(value, 0.0).astype(jnp.bfloat16)
        initial[position] = value
        even[pl.ds(pl.multiple_of((position + 1) * rows, rows), rows)] = value
    to_scalars.wait()

    order = {slot: index for index, slot in enumerate(slots)}

    def note(slot, index):
        if in_order:
            return plan[slot, index]
        found = plan[0, index]
        for which in range(1, parts):
            found = jnp.where(slot == slots[which], plan[which, index], found)
        return found

    for index, slot in enumerate(slots):
        position = slot_of(slot)
        before = slot_of(jnp.maximum(position - 1, 0))
        after = slot_of(jnp.minimum(position + 1, parts - 1))
        previous = [note(before, i) for i in range(listed_count)]
        following = [note(after, i) for i in range(listed_count)]
        band[position] = jnp.zeros(band.shape[1:], jnp.bfloat16)
        for block in range(blocks):
            for k in range(tile_count):
                source = plan[index, listed_count + block * tile_count + k]
                far = source - blocks
                column = blocks + source
                for i in range(listed_count):
                    column = jnp.where(far == i, previous[i], column)
                    column = jnp.where(far == listed_count + i, 2 * blocks + following[i], column)
                column = jnp.clip(column, 0, 3 * blocks - 1)
                start = pl.multiple_of(column * tile_rows, tile_rows)
                first = (block * tile_count + k) * tile_rows
                place = (position, slice(block * tile_rows, (block + 1) * tile_rows), pl.ds(start, tile_rows))
                band[place] += pieces[index][first : first + tile_rows]

    for index in range(len(inputs)):
        copy(index).wait()

    for layer in range(layers):
        beta = math.log(decay_theta / (layer + 1) + 1.0)
        reach = layers - 1 - layer
        count = min(parts, 2 * reach + 1)
        base = 0 if count == parts else jnp.clip(own - reach, 0, parts - count)
        before_ref, after_ref = states[layer % 2], states[(layer + 1) % 2]

        def advance(position, before_ref=before_ref, after_ref=after_ref, beta=beta, layer=layer):
            window = before_ref[pl.ds(pl.multiple_of(position * rows, rows), 3 * rows)]
            aggregate = jnp.dot(band[position], window, preferred_element_type=jnp.float32)
            support = (
                (1.0 - residual_share) * aggregate + residual_share * initial[position].astype(jnp.float32)
            ).astype(jnp.bfloat16)
            product = jnp.dot(support, layer_weight[layer], preferred_element_type=jnp.float32)
            mixed = (1.0 - beta) * support.astype(jnp.float32) + beta * product
            target = pl.ds(pl.multiple_of((position + 1) * rows, rows), rows)
            after_ref[target] = jnp.maximum(mixed, 0.0).astype(jnp.bfloat16)

        if in_order:
            pl.loop(base, base + count)(advance)
        else:
            for step in range(count):
                advance(base + step)
        if (layer + 1) % per_section == 0:
            leaving = layer // per_section
            mine = pl.ds(pl.multiple_of((own + 1) * rows, rows), rows)

            @pl.when(section == leaving)
            def _():
                placed_ref[0, group] = after_ref[mine]

            @pl.when(section ^ 1 == leaving)
            def _():
                sent_ref[...] = after_ref[mine]


def shards(features, input_weight, layer_weights, tiles, pub_ids, tile_src):
    groups, rows, _ = features.shape
    _, blocks, tile_count, tile_rows, _ = tiles.shape
    listed_count = pub_ids.shape[1]
    per_section, width, _ = layer_weights.shape
    section, sections = lax.axis_index("section"), lax.axis_size("section")
    me, doms = lax.axis_index("dom"), lax.axis_size("dom")
    layers = per_section * sections
    core, group = me % 2, section % groups

    half = width // 2
    my_share = lax.dynamic_slice_in_dim(layer_weights, core * half, half, 1)
    own_tiles = lax.dynamic_index_in_dim(tiles, group, 0, keepdims=False).reshape(-1, tile_rows)
    own_features = lax.dynamic_index_in_dim(features, group, 0, keepdims=False)
    own_ids = lax.dynamic_index_in_dim(pub_ids, group, 0, keepdims=False)
    own_sources = lax.dynamic_index_in_dim(tile_src, group, 0, keepdims=False).reshape(-1)
    notes = jnp.concatenate([own_ids, own_sources])
    notes = jnp.pad(notes.astype(jnp.bfloat16)[None], ((0, meta_rows - 1), (0, tile_rows - notes.shape[0])))
    payload = jnp.concatenate([own_tiles, own_features, notes], 0)
    payload, my_share = lax.optimization_barrier((payload, my_share))

    in_order = doms > layers or doms & (doms - 1) != 0
    lower = range(sections // 2)
    if in_order:
        parts, own = 2 * layers + 1, jnp.int32(layers)
        slots = tuple(range(parts))
        pieces = [payload if d == 0 else shifted(payload, "dom", d) for d in range(-layers, layers + 1)]
        first = pieces[0]
    else:
        parts, own = doms, me
        direct = {mask: swapped(payload, "dom", mask) for mask in reversed(range(2, parts, 2))}
        first = direct[2]
        slots, pieces = [0, 1], [payload, swapped(payload, "dom", 1)]
        for mask in range(2, parts, 2):
            slots += [mask, mask + 1]
            pieces += [direct[mask], swapped(direct[mask], "dom", 1)]
        slots = tuple(slots)
    received = []
    for mask in range(sections - 1, 1, -1):
        pairs = [(i, i ^ mask) for i in lower if i ^ mask not in lower]
        received.append((mask, one_way(my_share, "section", pairs)))
    later_share, _ = lax.optimization_barrier((my_share, first))
    received.append((1, swapped(later_share, "section", 1)))
    inputs, shares = [layer_weights], [(0, None)]
    for mask, share in received:
        inputs += [share, swapped(share, "dom", 1)]
        shares += [(mask, 0), (mask, 1)]
    place = jnp.stack([own, section, core, group]).astype(jnp.int32)

    dims = (
        parts, in_order, layers, per_section, blocks, tile_count, listed_count, tile_rows, rows, slots, tuple(shares),
    )
    smem = pl.BlockSpec(memory_space=pltpu.SMEM)
    vmem = pl.BlockSpec(memory_space=pltpu.VMEM)
    anywhere = pl.BlockSpec(memory_space=pl.ANY)
    placed, sent = pl.pallas_call(
        functools.partial(cone_kernel, dims),
        out_shape=(
            jax.ShapeDtypeStruct((1, groups, rows, width), jnp.bfloat16),
            jax.ShapeDtypeStruct((rows, width), jnp.bfloat16),
        ),
        in_specs=[smem, vmem] + [vmem] * parts + [anywhere] * len(inputs),
        out_specs=(vmem, vmem),
        scratch_shapes=[
            pltpu.VMEM((layers, width, width), jnp.bfloat16),
            pltpu.VMEM((parts, rows, 3 * rows), jnp.bfloat16),
            pltpu.VMEM((parts, rows, width), jnp.bfloat16),
            pltpu.VMEM(((parts + 2) * rows, width), jnp.bfloat16),
            pltpu.VMEM(((parts + 2) * rows, width), jnp.bfloat16),
            pltpu.VMEM((parts, tile_rows), jnp.int32),
            pltpu.SMEM((parts, tile_rows), jnp.int32),
            pltpu.SemaphoreType.DMA((len(inputs),)),
            pltpu.SemaphoreType.DMA,
        ],
        compiler_params=pltpu.CompilerParams(vmem_limit_bytes=vmem_bytes),
    )(place, input_weight, *pieces, *inputs)
    other = swapped(sent, "section", 1)
    return lax.dynamic_update_slice(placed, other[None, None], (0, 1 - group, 0, 0))


def solution(mesh):
    in_specs = (
        P(None, "dom", None),
        P(),
        P("section", None, None),
        P(None, "dom", None, None, None),
        P(None, "dom"),
        P(None, "dom", None),
    )
    out_specs = P("section", None, "dom", None)
    return jax.shard_map(shards, mesh=mesh, in_specs=in_specs, out_specs=out_specs, check_vma=False)
```

time: 177 us -> 87.5 us (0.49)
  the two profiles are of different devices: /device:TPU:13 before, /device:TPU:0 now
where the time goes in v1:
time: 87.5 us; the launch traced here: 87.3 us
  waiting for transfers between devices  41.1 us (47%)
  Pallas kernels  26.5 us (30%)
  starting transfers between devices  15.8 us (18%)
  local copies, waits for them, and re-layouts  3.58 us (4%)
    ppermute x12, waiting for transfers between devices, swapped(): lax.ppermute(block, axis, [(i, i ^ mask) for i in range(lax.axis_size(axi...  41.1 us
    pallas_call x1, Pallas kernels, shards(): pl.pallas_call(functools.partial(cone_kernel, dims), out_shape=(jax.Shape...  26.5 us
    ppermute x12, starting transfers between devices, swapped(): lax.ppermute(block, axis, [(i, i ^ mask) for i in range(lax.axis_size(axi...  10.2 us
    ppermute x2, starting transfers between devices, one_way(): return lax.ppermute(block, axis, pairs)  5.66 us
  transfers between devices with their start and end apart: 14, of which 7 were waited for; matrix products, arithmetic and copies ran while one was open for 0% of the time, Pallas kernels for 0%

profile of v1, /device:TPU:0, one launch (start us, length us, event | category | flops | bytes accessed | tf_op | source)
XLA Modules:
  0.0 87.3 jit_solution(4312757905834783711)
XLA Ops:
  0.0 0.7 copy-done.4
  0.7 0.0 copy-done.3
  0.8 0.1 concatenate.16
  0.9 0.8 dynamic-slice_bitcast_fusion
  1.7 0.1 fusion.5
  1.8 1.1 %constant_dynamic-slice_fusion = bf16[2,256,512]{2,1,0:T(8,128)(2,1)S(1)} fusion(bf16[2,512,512]{2,1,0:T(8,128)(2,1)} %refs_10_.1, s32[]{:T(128)S(6)} %select_n.30), kind=kLoop, calls=%fused_computation.11 | loop fusion | bytes 1048580 | tf_op jit(solution)/shard_map/dynamic_slice | solution.py:153
  3.0 0.0 copy-start.2
  3.0 3.1 %collective-permute-start.1 = (bf16[1312,128]{1,0:T(8,128)(2,1)S(1)}, bf16[1312,128]{1,0:T(8,128)(2,1)S(1)}, u32[]{:S(2)}, u32[]{:S(2)}) collective-permute-start(bf16[1312,128]{1,0:T(8,128)(2,1)S(1)} %pad_maximum_fusion.refs_2_), channel_id=1, source_target_pairs={{0,2},{1,3},{2,0},{3,1},{4,6},{5,7},{6,4},{7,5},{8,10},{9,11},{10,... | collective-permute-start | bytes 1007624 | tf_op jit(solution)/shard_map/ppermute | solution.py:18
  6.1 3.4 %collective-permute-start.9 = (bf16[2,256,512]{2,1,0:T(8,128)(2,1)S(1)}, bf16[2,256,512]{2,1,0:T(8,128)(2,1)S(1)}, u32[]{:S(2)}, u32[]{:S(2)}) collective-permute-start(bf16[2,256,512]{2,1,0:T(8,128)(2,1)S(1)} %constant_dynamic-slice_fusion), channel_id=1, source_target_pairs={{0,16},{8,24},{1,17},{9,25},{2,18},{10,26},{3,19},{11,27},{4,20},{... | collective-permute-start | bytes 1572872 | tf_op jit(solution)/shard_map/ppermute | solution.py:27
  9.6 2.2 %collective-permute-start.7 = (bf16[2,256,512]{2,1,0:T(8,128)(2,1)S(1)}, bf16[2,256,512]{2,1,0:T(8,128)(2,1)S(1)}, u32[]{:S(2)}, u32[]{:S(2)}) collective-permute-start(bf16[2,256,512]{2,1,0:T(8,128)(2,1)S(1)} %constant_dynamic-slice_fusion), channel_id=1, source_target_pairs={{0,24},{8,16},{1,25},{9,17},{2,26},{10,18},{3,27},{11,19},{4,28},{... | collective-permute-start | bytes 1572872 | tf_op jit(solution)/shard_map/ppermute | solution.py:27
  11.8 2.2 %collective-permute-done.1.refs_4_ = bf16[1312,128]{1,0:T(8,128)(2,1)S(1)} collective-permute-done((bf16[1312,128]{1,0:T(8,128)(2,1)S(1)}, bf16[1312,128]{1,0:T(8,128)(2,1)S(1)}, u32[]{:S(2)}, u32[]{:S(2)}) %collective-permute-start.1) | collective-permute-done | bytes 335904 | tf_op jit(solution)/shard_map/ppermute | solution.py:18
  14.0 1.7 %collective-permute-start.11 = (bf16[2,256,512]{2,1,0:T(8,128)(2,1)S(1)}, bf16[2,256,512]{2,1,0:T(8,128)(2,1)S(1)}, u32[]{:S(2)}, u32[]{:S(2)}) collective-permute-start(bf16[2,256,512]{2,1,0:T(8,128)(2,1)S(1)} %constant_dynamic-slice_fusion), channel_id=1, source_target_pairs={{0,8},{8,0},{16,24},{24,16},{1,9},{9,1},{17,25},{25,17},{2,10},{10... | collective-permute-start | bytes 1572872 | tf_op jit(solution)/shard_map/ppermute | solution.py:18
  15.6 3.6 %collective-permute-start.5 = (bf16[1312,128]{1,0:T(8,128)(2,1)S(1)}, bf16[1312,128]{1,0:T(8,128)(2,1)S(1)}, u32[]{:S(2)}, u32[]{:S(2)}) collective-permute-start(bf16[1312,128]{1,0:T(8,128)(2,1)S(1)} %pad_maximum_fusion.refs_2_), channel_id=1, source_target_pairs={{0,6},{1,7},{2,4},{3,5},{4,2},{5,3},{6,0},{7,1},{8,14},{9,15},{10,... | collective-permute-start | bytes 1007624 | tf_op jit(solution)/shard_map/ppermute | solution.py:18
  19.2 0.0 collective-permute-start.3
  19.3 9.1 %collective-permute-done.5.refs_8_ = bf16[1312,128]{1,0:T(8,128)(2,1)S(1)} collective-permute-done((bf16[1312,128]{1,0:T(8,128)(2,1)S(1)}, bf16[1312,128]{1,0:T(8,128)(2,1)S(1)}, u32[]{:S(2)}, u32[]{:S(2)}) %collective-permute-start.5) | collective-permute-done | bytes 335904 | tf_op jit(solution)/shard_map/ppermute | solution.py:18
  28.3 18.4 %collective-permute-done.3.refs_6_ = bf16[1312,128]{1,0:T(8,128)(2,1)S(1)} collective-permute-done((bf16[1312,128]{1,0:T(8,128)(2,1)S(1)}, bf16[1312,128]{1,0:T(8,128)(2,1)S(1)}, u32[]{:S(2)}, u32[]{:S(2)}) %collective-permute-start.3) | collective-permute-done | bytes 335904 | tf_op jit(solution)/shard_map/ppermute | solution.py:18
  46.7 0.0 collective-permute-done.9.refs_13_
  46.7 0.5 collective-permute-start.10
  47.2 0.0 collective-permute-done.7.refs_11_
  47.2 0.1 collective-permute-start.8
  47.3 0.4 collective-permute-start.12
  47.8 0.0 collective-permute-done.refs_3_
  47.8 0.1 collective-permute-start.4
  47.8 0.5 collective-permute-done.6.refs_9_
  48.4 0.1 collective-permute-start.2
  48.5 0.1 pad_add_fusion.refs_0_
  48.6 2.5 %collective-permute-done.4.refs_7_ = bf16[1312,128]{1,0:T(8,128)(2,1)S(1)} collective-permute-done((bf16[1312,128]{1,0:T(8,128)(2,1)S(1)}, bf16[1312,128]{1,0:T(8,128)(2,1)S(1)}, u32[]{:S(2)}, u32[]{:S(2)}) %collective-permute-start.4) | collective-permute-done | bytes 335904 | tf_op jit(solution)/shard_map/ppermute | solution.py:18
  51.1 0.5 collective-permute-done.2.refs_5_
  51.6 26.5 %shard_map.64 = (bf16[1,2,256,512]{3,2,1,0:T(8,128)(2,1)}, bf16[256,512]{1,0:T(8,128)(2,1)S(1)}) custom-call(s32[4]{0:T(128)S(1)} %pad_add_fusion.refs_0_, bf16[128,512]{1,0:T(8,128)(2,1)S(1)} %copy-done.2, bf16[1312,128]{1,0:T(8,128)(2,1)S(1)} %pad_maximum_fusion.refs_2_, bf16[1312,128]{1,0:T(8,128)(2,1)S(1)} %collective-permute-done.refs_3_, ...), custom_call_target="tpu_custom_call" | custom-call | tf_op jit(solution)/shard_map/pallas_call | solution.py:197
  78.1 0.6 collective-permute-start.13
  78.7 7.8 %collective-permute-done.13 = bf16[256,512]{1,0:T(8,128)(2,1)S(1)} collective-permute-done((bf16[256,512]{1,0:T(8,128)(2,1)S(1)}, bf16[256,512]{1,0:T(8,128)(2,1)S(1)}, u32[]{:S(2)}, u32[]{:S(2)}) %collective-permute-start.13) | collective-permute-done | bytes 262176 | tf_op jit(solution)/shard_map/ppermute | solution.py:18
  86.6 0.7 bitcast_dynamic-update-slice_fusion
  (17 shorter events, 0.1 us)
Async XLA Ops:
  0.0 1.7 %copy-start = (bf16[2,2,4,128,128]{4,3,2,1,0:T(8,128)(2,1)S(1)}, bf16[2,2,4,128,128]{4,3,2,1,0:T(8,128)(2,1)}, u32[]{:S(2)}) copy-start(bf16[2,2,4,128,128]{4,3,2,1,0:T(8,128)(2,1)} %param.9) | copy-start | bytes 1572868
  0.0 0.7 copy-start.4
  0.0 0.8 copy-start.3
  1.7 49.9 %copy-start.1 = (bf16[2,512,512]{2,1,0:T(8,128)(2,1)S(1)}, bf16[2,512,512]{2,1,0:T(8,128)(2,1)}, u32[]{:S(2)}) copy-start(bf16[2,512,512]{2,1,0:T(8,128)(2,1)} %refs_10_.1) | copy-start | bytes 3145732
  3.0 48.6 %copy-start.2 = (bf16[128,512]{1,0:T(8,128)(2,1)S(1)}, bf16[128,512]{1,0:T(8,128)(2,1)}, u32[]{:S(2)}) copy-start(bf16[128,512]{1,0:T(8,128)(2,1)} %refs_1_.1) | copy-start | bytes 393220
  3.0 11.0 %collective-permute-start.1 = (bf16[1312,128]{1,0:T(8,128)(2,1)S(1)}, bf16[1312,128]{1,0:T(8,128)(2,1)S(1)}, u32[]{:S(2)}, u32[]{:S(2)}) collective-permute-start(bf16[1312,128]{1,0:T(8,128)(2,1)S(1)} %pad_maximum_fusion.refs_2_), channel_id=1, source_target_pairs={{0,2},{1,3},{2,0},{3,1},{4,6},{5,7},{6,4},{7,5},{8,10},{9,11},{10,... | collective-permute-start | bytes 1007624 | tf_op jit(solution)/shard_map/ppermute | solution.py:18
  6.1 40.6 %collective-permute-start.9 = (bf16[2,256,512]{2,1,0:T(8,128)(2,1)S(1)}, bf16[2,256,512]{2,1,0:T(8,128)(2,1)S(1)}, u32[]{:S(2)}, u32[]{:S(2)}) collective-permute-start(bf16[2,256,512]{2,1,0:T(8,128)(2,1)S(1)} %constant_dynamic-slice_fusion), channel_id=1, source_target_pairs={{0,16},{8,24},{1,17},{9,25},{2,18},{10,26},{3,19},{11,27},{4,20},{... | collective-permute-start | bytes 1572872 | tf_op jit(solution)/shard_map/ppermute | solution.py:27
  9.6 37.7 %collective-permute-start.7 = (bf16[2,256,512]{2,1,0:T(8,128)(2,1)S(1)}, bf16[2,256,512]{2,1,0:T(8,128)(2,1)S(1)}, u32[]{:S(2)}, u32[]{:S(2)}) collective-permute-start(bf16[2,256,512]{2,1,0:T(8,128)(2,1)S(1)} %constant_dynamic-slice_fusion), channel_id=1, source_target_pairs={{0,24},{8,16},{1,25},{9,17},{2,26},{10,18},{3,27},{11,19},{4,28},{... | collective-permute-start | bytes 1572872 | tf_op jit(solution)/shard_map/ppermute | solution.py:27
  14.0 33.3 %collective-permute-start.11 = (bf16[2,256,512]{2,1,0:T(8,128)(2,1)S(1)}, bf16[2,256,512]{2,1,0:T(8,128)(2,1)S(1)}, u32[]{:S(2)}, u32[]{:S(2)}) collective-permute-start(bf16[2,256,512]{2,1,0:T(8,128)(2,1)S(1)} %constant_dynamic-slice_fusion), channel_id=1, source_target_pairs={{0,8},{8,0},{16,24},{24,16},{1,9},{9,1},{17,25},{25,17},{2,10},{10... | collective-permute-start | bytes 1572872 | tf_op jit(solution)/shard_map/ppermute | solution.py:18
  15.6 12.7 %collective-permute-start.5 = (bf16[1312,128]{1,0:T(8,128)(2,1)S(1)}, bf16[1312,128]{1,0:T(8,128)(2,1)S(1)}, u32[]{:S(2)}, u32[]{:S(2)}) collective-permute-start(bf16[1312,128]{1,0:T(8,128)(2,1)S(1)} %pad_maximum_fusion.refs_2_), channel_id=1, source_target_pairs={{0,6},{1,7},{2,4},{3,5},{4,2},{5,3},{6,0},{7,1},{8,14},{9,15},{10,... | collective-permute-start | bytes 1007624 | tf_op jit(solution)/shard_map/ppermute | solution.py:18
  19.2 27.5 %collective-permute-start.3 = (bf16[1312,128]{1,0:T(8,128)(2,1)S(1)}, bf16[1312,128]{1,0:T(8,128)(2,1)S(1)}, u32[]{:S(2)}, u32[]{:S(2)}) collective-permute-start(bf16[1312,128]{1,0:T(8,128)(2,1)S(1)} %pad_maximum_fusion.refs_2_), channel_id=1, source_target_pairs={{0,4},{1,5},{2,6},{3,7},{4,0},{5,1},{6,2},{7,3},{8,12},{9,13},{10,... | collective-permute-start | bytes 1007624 | tf_op jit(solution)/shard_map/ppermute | solution.py:18
  28.3 19.4 %collective-permute-start = (bf16[1312,128]{1,0:T(8,128)(2,1)S(1)}, bf16[1312,128]{1,0:T(8,128)(2,1)S(1)}, u32[]{:S(2)}, u32[]{:S(2)}) collective-permute-start(bf16[1312,128]{1,0:T(8,128)(2,1)S(1)} %pad_maximum_fusion.refs_2_), channel_id=1, source_target_pairs={{0,1},{1,0},{2,3},{3,2},{4,5},{5,4},{6,7},{7,6},{8,9},{9,8},{10,11... | collective-permute-start | bytes 1007624 | tf_op jit(solution)/shard_map/ppermute | solution.py:18
  46.7 1.6 %collective-permute-start.6 = (bf16[1312,128]{1,0:T(8,128)(2,1)S(1)}, bf16[1312,128]{1,0:T(8,128)(2,1)S(1)}, u32[]{:S(2)}, u32[]{:S(2)}) collective-permute-start(bf16[1312,128]{1,0:T(8,128)(2,1)S(1)} %collective-permute-done.5.refs_8_), channel_id=1, source_target_pairs={{0,1},{1,0},{2,3},{3,2},{4,5},{5,4},{6,7},{7,6},{8,9},{9,8},{10,11... | collective-permute-start | bytes 1007624 | tf_op jit(solution)/shard_map/ppermute | solution.py:18
  46.7 4.8 %collective-permute-start.10 = (bf16[2,256,512]{2,1,0:T(8,128)(2,1)S(1)}, bf16[2,256,512]{2,1,0:T(8,128)(2,1)S(1)}, u32[]{:S(2)}, u32[]{:S(2)}) collective-permute-start(bf16[2,256,512]{2,1,0:T(8,128)(2,1)S(1)} %collective-permute-done.9.refs_13_), channel_id=1, source_target_pairs={{0,1},{1,0},{2,3},{3,2},{4,5},{5,4},{6,7},{7,6},{8,9},{9,8},{10,11... | collective-permute-start | bytes 1572872 | tf_op jit(solution)/shard_map/ppermute | solution.py:18
  47.2 4.3 %collective-permute-start.8 = (bf16[2,256,512]{2,1,0:T(8,128)(2,1)S(1)}, bf16[2,256,512]{2,1,0:T(8,128)(2,1)S(1)}, u32[]{:S(2)}, u32[]{:S(2)}) collective-permute-start(bf16[2,256,512]{2,1,0:T(8,128)(2,1)S(1)} %collective-permute-done.7.refs_11_), channel_id=1, source_target_pairs={{0,1},{1,0},{2,3},{3,2},{4,5},{5,4},{6,7},{7,6},{8,9},{9,8},{10,11... | collective-permute-start | bytes 1572872 | tf_op jit(solution)/shard_map/ppermute | solution.py:18
  47.3 4.3 %collective-permute-start.12 = (bf16[2,256,512]{2,1,0:T(8,128)(2,1)S(1)}, bf16[2,256,512]{2,1,0:T(8,128)(2,1)S(1)}, u32[]{:S(2)}, u32[]{:S(2)}) collective-permute-start(bf16[2,256,512]{2,1,0:T(8,128)(2,1)S(1)} %collective-permute-done.11.refs_15_), channel_id=1, source_target_pairs={{0,1},{1,0},{2,3},{3,2},{4,5},{5,4},{6,7},{7,6},{8,9},{9,8},{10,11... | collective-permute-start | bytes 1572872 | tf_op jit(solution)/shard_map/ppermute | solution.py:18
  47.8 3.3 %collective-permute-start.4 = (bf16[1312,128]{1,0:T(8,128)(2,1)S(1)}, bf16[1312,128]{1,0:T(8,128)(2,1)S(1)}, u32[]{:S(2)}, u32[]{:S(2)}) collective-permute-start(bf16[1312,128]{1,0:T(8,128)(2,1)S(1)} %collective-permute-done.3.refs_6_), channel_id=1, source_target_pairs={{0,1},{1,0},{2,3},{3,2},{4,5},{5,4},{6,7},{7,6},{8,9},{9,8},{10,11... | collective-permute-start | bytes 1007624 | tf_op jit(solution)/shard_map/ppermute | solution.py:18
  48.4 3.2 %collective-permute-start.2 = (bf16[1312,128]{1,0:T(8,128)(2,1)S(1)}, bf16[1312,128]{1,0:T(8,128)(2,1)S(1)}, u32[]{:S(2)}, u32[]{:S(2)}) collective-permute-start(bf16[1312,128]{1,0:T(8,128)(2,1)S(1)} %collective-permute-done.1.refs_4_), channel_id=1, source_target_pairs={{0,1},{1,0},{2,3},{3,2},{4,5},{5,4},{6,7},{7,6},{8,9},{9,8},{10,11... | collective-permute-start | bytes 1007624 | tf_op jit(solution)/shard_map/ppermute | solution.py:18
  78.1 8.4 %collective-permute-start.13 = (bf16[256,512]{1,0:T(8,128)(2,1)S(1)}, bf16[256,512]{1,0:T(8,128)(2,1)S(1)}, u32[]{:S(2)}, u32[]{:S(2)}) collective-permute-start(bf16[256,512]{1,0:T(8,128)(2,1)S(1)} %get-tuple-element.14), channel_id=1, source_target_pairs={{0,8},{8,0},{16,24},{24,16},{1,9},{9,1},{17,25},{25,17},{2,10},{10... | collective-permute-start | bytes 786440 | tf_op jit(solution)/shard_map/ppermute | solution.py:18

commit v2 on v1

--- a/solution.py
+++ b/solution.py
@@ -11,7 +11,7 @@
 residual_share = 0.1
 decay_theta = 0.5
 vmem_bytes = 44 * 2**20
-meta_rows = 32
+meta_rows = 16
 
 
 def swapped(block, axis, mask):
@@ -28,22 +28,28 @@
 
 
 def cone_kernel(dims, *refs):
-    (parts, in_order, layers, per_section, blocks, tile_count, listed_count, tile_rows, rows, slots, shares) = dims
+    (parts, in_order, layers, per_section, blocks, tile_count, listed_count, tile_rows, rows, slots, shares, lower) = dims
     place_ref, entry_ref = refs[:2]
     pieces = refs[2 : 2 + parts]
     inputs = refs[2 + parts : 2 + parts + len(shares)]
     placed_ref, sent_ref = refs[2 + parts + len(shares) : 4 + parts + len(shares)]
-    layer_weight, band, initial, even, odd, notes, plan, sems, plan_sem = refs[4 + parts + len(shares) :]
+    layer_weight, band, initial, even, odd, first_support, second_support, notes, plan, sems, plan_sem = refs[4 + parts + len(shares) :]
     own, section, core, group = [place_ref[i] for i in range(4)]
     states = (even, odd)
     tile_area = blocks * tile_count * tile_rows
 
     def copy(index):
-        mask, flip = shares[index]
-        target = layer_weight.at[pl.ds((section ^ mask) * per_section, per_section)]
-        if flip is not None:
-            size = inputs[index].shape[1]
-            target = target.at[:, pl.ds(pl.multiple_of((core ^ flip) * size, size), size)]
+        kind, flip = shares[index]
+        if kind == "up":
+            place = ((section ^ core) & 1) ^ flip
+            place = jnp.where(section < lower, lower + place, place)
+            target = layer_weight.at[pl.ds(place * per_section, per_section)]
+        else:
+            owner = section ^ 1 if kind == "pair" else section
+            target = layer_weight.at[pl.ds(owner * per_section, per_section)]
+            if flip is not None:
+                size = inputs[index].shape[1]
+                target = target.at[:, pl.ds(pl.multiple_of((core ^ flip) * size, size), size)]
         return pltpu.make_async_copy(inputs[index], target, sems.at[index])
 
     for index in range(len(inputs)):
@@ -100,32 +106,77 @@
                 place = (position, slice(block * tile_rows, (block + 1) * tile_rows), pl.ds(start, tile_rows))
                 band[place] += pieces[index][first : first + tile_rows]
 
-    for index in range(len(inputs)):
-        copy(index).wait()
-
+    raised = [index for index, share in enumerate(shares) if share[0] == "up"]
+    homes = [index for index, share in enumerate(shares) if share[0] != "up"]
+
+    @pl.when(section >= lower)
+    def _():
+        for index in raised:
+            copy(index).wait()
+
+    @pl.when(section < lower)
+    def _():
+        for index in homes:
+            copy(index).wait()
+
+    depth = jnp.where(section < lower, lower * per_section, layers)
     for layer in range(layers):
         beta = math.log(decay_theta / (layer + 1) + 1.0)
-        reach = layers - 1 - layer
-        count = min(parts, 2 * reach + 1)
-        base = 0 if count == parts else jnp.clip(own - reach, 0, parts - count)
+        reach = depth - 1 - layer
+        lowest = jnp.maximum(own - reach, 0)
+        highest = jnp.minimum(own + reach + 1, parts)
+        count = jnp.where(reach >= 0, highest - lowest, 0)
         before_ref, after_ref = states[layer % 2], states[(layer + 1) % 2]
-
-        def advance(position, before_ref=before_ref, after_ref=after_ref, beta=beta, layer=layer):
+        if layer == lower * per_section:
+
+            @pl.when(section >= lower)
+            def _():
+                for index in homes:
+                    copy(index).wait()
+
+            @pl.when(section < lower)
+            def _():
+                for index in raised:
+                    copy(index).wait()
+
+        def support_of(position, before_ref=before_ref):
             window = before_ref[pl.ds(pl.multiple_of(position * rows, rows), 3 * rows)]
             aggregate = jnp.dot(band[position], window, preferred_element_type=jnp.float32)
-            support = (
+            return (
                 (1.0 - residual_share) * aggregate + residual_share * initial[position].astype(jnp.float32)
             ).astype(jnp.bfloat16)
+
+        def finish(position, support, after_ref=after_ref, beta=beta, layer=layer):
             product = jnp.dot(support, layer_weight[layer], preferred_element_type=jnp.float32)
             mixed = (1.0 - beta) * support.astype(jnp.float32) + beta * product
             target = pl.ds(pl.multiple_of((position + 1) * rows, rows), rows)
             after_ref[target] = jnp.maximum(mixed, 0.0).astype(jnp.bfloat16)
 
-        if in_order:
-            pl.loop(base, base + count)(advance)
-        else:
-            for step in range(count):
-                advance(base + step)
+        partial = count > 0
+        if not in_order and 2 * (layers - 1 - layer) + 1 >= parts:
+            partial = partial & (count < parts)
+
+            @pl.when(count == parts)
+            def _(support_of=support_of, finish=finish):
+                for position in range(parts):
+                    finish(position, support_of(position))
+
+        @pl.when(partial)
+        def _(support_of=support_of, finish=finish, lowest=lowest, highest=highest, count=count):
+            first_support[...] = support_of(lowest)
+
+            @pl.loop(0, count // 2)
+            def _(pair):
+                position = lowest + 2 * pair
+                second_support[...] = support_of(position + 1)
+                finish(position, first_support[...])
+                first_support[...] = support_of(jnp.minimum(position + 2, highest - 1))
+                finish(position + 1, second_support[...])
+
+            @pl.when(count % 2 == 1)
+            def _():
+                finish(highest - 1, first_support[...])
+
         if (layer + 1) % per_section == 0:
             leaving = layer // per_section
             mine = pl.ds(pl.multiple_of((own + 1) * rows, rows), rows)
@@ -149,8 +200,6 @@
     layers = per_section * sections
     core, group = me % 2, section % groups
 
-    half = width // 2
-    my_share = lax.dynamic_slice_in_dim(layer_weights, core * half, half, 1)
     own_tiles = lax.dynamic_index_in_dim(tiles, group, 0, keepdims=False).reshape(-1, tile_rows)
     own_features = lax.dynamic_index_in_dim(features, group, 0, keepdims=False)
     own_ids = lax.dynamic_index_in_dim(pub_ids, group, 0, keepdims=False)
@@ -158,38 +207,37 @@
     notes = jnp.concatenate([own_ids, own_sources])
     notes = jnp.pad(notes.astype(jnp.bfloat16)[None], ((0, meta_rows - 1), (0, tile_rows - notes.shape[0])))
     payload = jnp.concatenate([own_tiles, own_features, notes], 0)
-    payload, my_share = lax.optimization_barrier((payload, my_share))
+    payload, layer_weights = lax.optimization_barrier((payload, layer_weights))
 
     in_order = doms > layers or doms & (doms - 1) != 0
-    lower = range(sections // 2)
+    lower = sections // 2
+    senders = [(t, d) for t in range(lower) for d in range(doms)]
+    route = [(t * doms + d, (lower + (t ^ d % 2)) * doms + d) for t, d in senders]
+    half = width // 2
+    my_share = lax.dynamic_slice_in_dim(layer_weights, core * half, half, 1)
+    masks = () if in_order else range(2, doms, 2)
+    far = [swapped(payload, "dom", mask) for mask in masks]
+    up = one_way(layer_weights, ("section", "dom"), route)
+    pair = swapped(my_share, "section", 1)
+    mate = swapped(payload, "dom", 1)
+    far, up, pair, mate = lax.optimization_barrier((far, up, pair, mate))
     if in_order:
         parts, own = 2 * layers + 1, jnp.int32(layers)
         slots = tuple(range(parts))
         pieces = [payload if d == 0 else shifted(payload, "dom", d) for d in range(-layers, layers + 1)]
-        first = pieces[0]
     else:
         parts, own = doms, me
-        direct = {mask: swapped(payload, "dom", mask) for mask in reversed(range(2, parts, 2))}
-        first = direct[2]
-        slots, pieces = [0, 1], [payload, swapped(payload, "dom", 1)]
-        for mask in range(2, parts, 2):
+        slots, pieces = [0, 1], [payload, mate]
+        for mask, piece in zip(masks, far):
             slots += [mask, mask + 1]
-            pieces += [direct[mask], swapped(direct[mask], "dom", 1)]
+            pieces += [piece, swapped(piece, "dom", 1)]
         slots = tuple(slots)
-    received = []
-    for mask in range(sections - 1, 1, -1):
-        pairs = [(i, i ^ mask) for i in lower if i ^ mask not in lower]
-        received.append((mask, one_way(my_share, "section", pairs)))
-    later_share, _ = lax.optimization_barrier((my_share, first))
-    received.append((1, swapped(later_share, "section", 1)))
-    inputs, shares = [layer_weights], [(0, None)]
-    for mask, share in received:
-        inputs += [share, swapped(share, "dom", 1)]
-        shares += [(mask, 0), (mask, 1)]
+    inputs = [layer_weights, up, swapped(up, "dom", 1), pair, swapped(pair, "dom", 1)]
+    shares = [("own", None), ("up", 0), ("up", 1), ("pair", 0), ("pair", 1)]
     place = jnp.stack([own, section, core, group]).astype(jnp.int32)
 
     dims = (
-        parts, in_order, layers, per_section, blocks, tile_count, listed_count, tile_rows, rows, slots, tuple(shares),
+        parts, in_order, layers, per_section, blocks, tile_count, listed_count, tile_rows, rows, slots, tuple(shares), lower,
     )
     smem = pl.BlockSpec(memory_space=pltpu.SMEM)
     vmem = pl.BlockSpec(memory_space=pltpu.VMEM)
@@ -208,6 +256,8 @@
             pltpu.VMEM((parts, rows, width), jnp.bfloat16),
             pltpu.VMEM(((parts + 2) * rows, width), jnp.bfloat16),
             pltpu.VMEM(((parts + 2) * rows, width), jnp.bfloat16),
+            pltpu.VMEM((rows, width), jnp.bfloat16),
+            pltpu.VMEM((rows, width), jnp.bfloat16),
             pltpu.VMEM((parts, tile_rows), jnp.int32),
             pltpu.SMEM((parts, tile_rows), jnp.int32),
             pltpu.SemaphoreType.DMA((len(inputs),)),

time: 87.5 us -> 77.6 us (0.89)
  the two profiles are of different devices: /device:TPU:0 before, /device:TPU:13 now
where the time goes in v2:
time: 77.6 us; the launch traced here: 77.4 us
  waiting for transfers between devices  37.2 us (48%)
  Pallas kernels  27.4 us (35%)
  starting transfers between devices  9.37 us (12%)
  local copies, waits for them, and re-layouts  1.71 us (2%)
  other arithmetic  1.66 us (2%)
    ppermute x11, waiting for transfers between devices, swapped(): lax.ppermute(block, axis, [(i, i ^ mask) for i in range(lax.axis_size(axi...  37.2 us
    pallas_call x1, Pallas kernels, shards(): pl.pallas_call(functools.partial(cone_kernel, dims), out_shape=(jax.Shape...  27.4 us
    ppermute x11, starting transfers between devices, swapped(): lax.ppermute(block, axis, [(i, i ^ mask) for i in range(lax.axis_size(axi...  8.08 us
  transfers between devices with their start and end apart: 12, of which 6 were waited for; matrix products, arithmetic and copies ran while one was open for 0% of the time, Pallas kernels for 0%

profile of v2, /device:TPU:13, one launch (start us, length us, event | category | flops | bytes accessed | tf_op | source)
XLA Modules:
  0.0 77.4 jit_solution(2440798775113591980)
XLA Ops:
  0.0 0.8 %fusion.7 = bf16[1,2]{1,0:T(2,128)(2,1)S(1)} fusion(s32[2,2]{1,0:T(2,128)} %param.10, s32[]{:T(128)S(6)} %select_n.29), kind=kLoop, calls=%fused_computation.16 | loop fusion | flops 2 | bytes 16 | tf_op jit(solution)/shard_map/convert
  0.8 0.7 fusion.6
  1.5 0.1 concatenate.16
  1.6 0.8 %dynamic-slice_bitcast_fusion = bf16[256,128]{1,0:T(8,128)(2,1)S(1)} fusion(bf16[2,256,128]{2,1,0:T(8,128)(2,1)} %param.6, s32[]{:T(128)S(6)} %select_n.29), kind=kLoop, calls=%fused_computation.2 | loop fusion | bytes 131076 | tf_op jit(solution)/shard_map/jit(dynamic_index_in_dim)/squeeze | solution.py:204
  2.4 0.1 fusion.5
  2.6 1.3 %collective-permute-start.3 = (bf16[2,512,512]{2,1,0:T(8,128)(2,1)S(1)}, bf16[2,512,512]{2,1,0:T(8,128)(2,1)S(1)}, u32[]{:S(2)}, u32[]{:S(2)}) collective-permute-start(bf16[2,512,512]{2,1,0:T(8,128)(2,1)S(1)} %copy-done.1), channel_id=1, source_target_pairs={{0,16},{1,25},{2,18},{3,27},{4,20},{5,29},{6,22},{7,31},{8,24},{9,... | collective-permute-start | bytes 3145736 | tf_op jit(solution)/shard_map/ppermute | solution.py:27
  3.9 0.7 collective-permute-start.5
  4.6 1.3 %collective-permute-start.4 = (bf16[2,256,512]{2,1,0:T(8,128)(2,1)S(1)}, bf16[2,256,512]{2,1,0:T(8,128)(2,1)S(1)}, u32[]{:S(2)}, u32[]{:S(2)}) collective-permute-start(bf16[2,256,512]{2,1,0:T(8,128)(2,1)S(1)} %constant_dynamic-slice_fusion), channel_id=1, source_target_pairs={{0,8},{8,0},{16,24},{24,16},{1,9},{9,1},{17,25},{25,17},{2,10},{10... | collective-permute-start | bytes 1572872 | tf_op jit(solution)/shard_map/ppermute | solution.py:18
  5.9 1.3 %collective-permute-start.2 = (bf16[1296,128]{1,0:T(8,128)(2,1)S(1)}, bf16[1296,128]{1,0:T(8,128)(2,1)S(1)}, u32[]{:S(2)}, u32[]{:S(2)}) collective-permute-start(bf16[1296,128]{1,0:T(8,128)(2,1)S(1)} %pad_maximum_fusion.refs_2_), channel_id=1, source_target_pairs={{0,6},{1,7},{2,4},{3,5},{4,2},{5,3},{6,0},{7,1},{8,14},{9,15},{10,... | collective-permute-start | bytes 995336 | tf_op jit(solution)/shard_map/ppermute | solution.py:18
  7.2 1.0 %collective-permute-start.1 = (bf16[1296,128]{1,0:T(8,128)(2,1)S(1)}, bf16[1296,128]{1,0:T(8,128)(2,1)S(1)}, u32[]{:S(2)}, u32[]{:S(2)}) collective-permute-start(bf16[1296,128]{1,0:T(8,128)(2,1)S(1)} %pad_maximum_fusion.refs_2_), channel_id=1, source_target_pairs={{0,4},{1,5},{2,6},{3,7},{4,0},{5,1},{6,2},{7,3},{8,12},{9,13},{10,... | collective-permute-start | bytes 995336 | tf_op jit(solution)/shard_map/ppermute | solution.py:18
  8.2 0.0 collective-permute-done.5.refs_3_
  8.2 1.2 %collective-permute-start = (bf16[1296,128]{1,0:T(8,128)(2,1)S(1)}, bf16[1296,128]{1,0:T(8,128)(2,1)S(1)}, u32[]{:S(2)}, u32[]{:S(2)}) collective-permute-start(bf16[1296,128]{1,0:T(8,128)(2,1)S(1)} %pad_maximum_fusion.refs_2_), channel_id=1, source_target_pairs={{0,2},{1,3},{2,0},{3,1},{4,6},{5,7},{6,4},{7,5},{8,10},{9,11},{10,... | collective-permute-start | bytes 995336 | tf_op jit(solution)/shard_map/ppermute | solution.py:18
  9.4 19.8 %collective-permute-done.2.refs_8_ = bf16[1296,128]{1,0:T(8,128)(2,1)S(1)} collective-permute-done((bf16[1296,128]{1,0:T(8,128)(2,1)S(1)}, bf16[1296,128]{1,0:T(8,128)(2,1)S(1)}, u32[]{:S(2)}, u32[]{:S(2)}) %collective-permute-start.2) | collective-permute-done | bytes 331808 | tf_op jit(solution)/shard_map/ppermute | solution.py:18
  29.2 6.2 %collective-permute-done.1.refs_6_ = bf16[1296,128]{1,0:T(8,128)(2,1)S(1)} collective-permute-done((bf16[1296,128]{1,0:T(8,128)(2,1)S(1)}, bf16[1296,128]{1,0:T(8,128)(2,1)S(1)}, u32[]{:S(2)}, u32[]{:S(2)}) %collective-permute-start.1) | collective-permute-done | bytes 331808 | tf_op jit(solution)/shard_map/ppermute | solution.py:18
  35.4 0.0 collective-permute-done.refs_4_
  35.4 0.0 collective-permute-done.4.refs_13_
  35.4 0.0 collective-permute-done.3.refs_11_
  35.4 1.2 %collective-permute-start.9 = (bf16[2,512,512]{2,1,0:T(8,128)(2,1)S(1)}, bf16[2,512,512]{2,1,0:T(8,128)(2,1)S(1)}, u32[]{:S(2)}, u32[]{:S(2)}) collective-permute-start(bf16[2,512,512]{2,1,0:T(8,128)(2,1)S(1)} %collective-permute-done.3.refs_11_), channel_id=1, source_target_pairs={{0,1},{1,0},{2,3},{3,2},{4,5},{5,4},{6,7},{7,6},{8,9},{9,8},{10,11... | collective-permute-start | bytes 3145736 | tf_op jit(solution)/shard_map/ppermute | solution.py:18
  36.6 0.1 collective-permute-start.10
  36.7 0.4 collective-permute-start.6
  37.1 0.1 collective-permute-start.7
  37.2 0.4 collective-permute-start.8
  37.7 0.1 pad_add_fusion.refs_0_
  37.7 2.4 %collective-permute-done.6.refs_5_ = bf16[1296,128]{1,0:T(8,128)(2,1)S(1)} collective-permute-done((bf16[1296,128]{1,0:T(8,128)(2,1)S(1)}, bf16[1296,128]{1,0:T(8,128)(2,1)S(1)}, u32[]{:S(2)}, u32[]{:S(2)}) %collective-permute-start.6) | collective-permute-done | bytes 331808 | tf_op jit(solution)/shard_map/ppermute | solution.py:18
  40.1 0.5 collective-permute-done.7.refs_7_
  40.6 0.5 collective-permute-done.8.refs_9_
  41.1 0.0 collective-permute-done.10.refs_14_
  41.1 0.0 collective-permute-done.9.refs_12_
  41.1 27.4 %shard_map.64 = (bf16[1,2,256,512]{3,2,1,0:T(8,128)(2,1)}, bf16[256,512]{1,0:T(8,128)(2,1)S(1)}) custom-call(s32[4]{0:T(128)S(1)} %pad_add_fusion.refs_0_, bf16[128,512]{1,0:T(8,128)(2,1)S(1)} %copy-done.2, bf16[1296,128]{1,0:T(8,128)(2,1)S(1)} %pad_maximum_fusion.refs_2_, bf16[1296,128]{1,0:T(8,128)(2,1)S(1)} %collective-permute-done.5.refs_3_, ...), custom_call_target="tpu_custom_call" | custom-call | tf_op jit(solution)/shard_map/pallas_call | solution.py:245
  68.5 0.3 collective-permute-start.11
  68.8 7.8 %collective-permute-done.11 = bf16[256,512]{1,0:T(8,128)(2,1)S(1)} collective-permute-done((bf16[256,512]{1,0:T(8,128)(2,1)S(1)}, bf16[256,512]{1,0:T(8,128)(2,1)S(1)}, u32[]{:S(2)}, u32[]{:S(2)}) %collective-permute-start.11) | collective-permute-done | bytes 262176 | tf_op jit(solution)/shard_map/ppermute | solution.py:18
  76.6 0.7 bitcast_dynamic-update-slice_fusion
  (9 shorter events, 0.1 us)
Async XLA Ops:
  0.0 2.4 %copy-start = (bf16[2,2,4,128,128]{4,3,2,1,0:T(8,128)(2,1)S(1)}, bf16[2,2,4,128,128]{4,3,2,1,0:T(8,128)(2,1)}, u32[]{:S(2)}) copy-start(bf16[2,2,4,128,128]{4,3,2,1,0:T(8,128)(2,1)} %param.9) | copy-start | bytes 1572868
  0.0 2.6 %copy-start.1 = (bf16[2,512,512]{2,1,0:T(8,128)(2,1)S(1)}, bf16[2,512,512]{2,1,0:T(8,128)(2,1)}, u32[]{:S(2)}) copy-start(bf16[2,512,512]{2,1,0:T(8,128)(2,1)} %refs_10_) | copy-start | bytes 3145732
  2.6 32.8 %collective-permute-start.3 = (bf16[2,512,512]{2,1,0:T(8,128)(2,1)S(1)}, bf16[2,512,512]{2,1,0:T(8,128)(2,1)S(1)}, u32[]{:S(2)}, u32[]{:S(2)}) collective-permute-start(bf16[2,512,512]{2,1,0:T(8,128)(2,1)S(1)} %copy-done.1), channel_id=1, source_target_pairs={{0,16},{1,25},{2,18},{3,27},{4,20},{5,29},{6,22},{7,31},{8,24},{9,... | collective-permute-start | bytes 3145736 | tf_op jit(solution)/shard_map/ppermute | solution.py:27
  3.9 4.4 %collective-permute-start.5 = (bf16[1296,128]{1,0:T(8,128)(2,1)S(1)}, bf16[1296,128]{1,0:T(8,128)(2,1)S(1)}, u32[]{:S(2)}, u32[]{:S(2)}) collective-permute-start(bf16[1296,128]{1,0:T(8,128)(2,1)S(1)} %pad_maximum_fusion.refs_2_), channel_id=1, source_target_pairs={{0,1},{1,0},{2,3},{3,2},{4,5},{5,4},{6,7},{7,6},{8,9},{9,8},{10,11... | collective-permute-start | bytes 995336 | tf_op jit(solution)/shard_map/ppermute | solution.py:18
  4.6 36.5 %copy-start.2 = (bf16[128,512]{1,0:T(8,128)(2,1)S(1)}, bf16[128,512]{1,0:T(8,128)(2,1)}, u32[]{:S(2)}) copy-start(bf16[128,512]{1,0:T(8,128)(2,1)} %refs_1_.1) | copy-start | bytes 393220
  4.6 30.8 %collective-permute-start.4 = (bf16[2,256,512]{2,1,0:T(8,128)(2,1)S(1)}, bf16[2,256,512]{2,1,0:T(8,128)(2,1)S(1)}, u32[]{:S(2)}, u32[]{:S(2)}) collective-permute-start(bf16[2,256,512]{2,1,0:T(8,128)(2,1)S(1)} %constant_dynamic-slice_fusion), channel_id=1, source_target_pairs={{0,8},{8,0},{16,24},{24,16},{1,9},{9,1},{17,25},{25,17},{2,10},{10... | collective-permute-start | bytes 1572872 | tf_op jit(solution)/shard_map/ppermute | solution.py:18
  5.9 23.3 %collective-permute-start.2 = (bf16[1296,128]{1,0:T(8,128)(2,1)S(1)}, bf16[1296,128]{1,0:T(8,128)(2,1)S(1)}, u32[]{:S(2)}, u32[]{:S(2)}) collective-permute-start(bf16[1296,128]{1,0:T(8,128)(2,1)S(1)} %pad_maximum_fusion.refs_2_), channel_id=1, source_target_pairs={{0,6},{1,7},{2,4},{3,5},{4,2},{5,3},{6,0},{7,1},{8,14},{9,15},{10,... | collective-permute-start | bytes 995336 | tf_op jit(solution)/shard_map/ppermute | solution.py:18
  7.2 28.2 %collective-permute-start.1 = (bf16[1296,128]{1,0:T(8,128)(2,1)S(1)}, bf16[1296,128]{1,0:T(8,128)(2,1)S(1)}, u32[]{:S(2)}, u32[]{:S(2)}) collective-permute-start(bf16[1296,128]{1,0:T(8,128)(2,1)S(1)} %pad_maximum_fusion.refs_2_), channel_id=1, source_target_pairs={{0,4},{1,5},{2,6},{3,7},{4,0},{5,1},{6,2},{7,3},{8,12},{9,13},{10,... | collective-permute-start | bytes 995336 | tf_op jit(solution)/shard_map/ppermute | solution.py:18
  8.2 27.2 %collective-permute-start = (bf16[1296,128]{1,0:T(8,128)(2,1)S(1)}, bf16[1296,128]{1,0:T(8,128)(2,1)S(1)}, u32[]{:S(2)}, u32[]{:S(2)}) collective-permute-start(bf16[1296,128]{1,0:T(8,128)(2,1)S(1)} %pad_maximum_fusion.refs_2_), channel_id=1, source_target_pairs={{0,2},{1,3},{2,0},{3,1},{4,6},{5,7},{6,4},{7,5},{8,10},{9,11},{10,... | collective-permute-start | bytes 995336 | tf_op jit(solution)/shard_map/ppermute | solution.py:18
  35.4 5.7 %collective-permute-start.9 = (bf16[2,512,512]{2,1,0:T(8,128)(2,1)S(1)}, bf16[2,512,512]{2,1,0:T(8,128)(2,1)S(1)}, u32[]{:S(2)}, u32[]{:S(2)}) collective-permute-start(bf16[2,512,512]{2,1,0:T(8,128)(2,1)S(1)} %collective-permute-done.3.refs_11_), channel_id=1, source_target_pairs={{0,1},{1,0},{2,3},{3,2},{4,5},{5,4},{6,7},{7,6},{8,9},{9,8},{10,11... | collective-permute-start | bytes 3145736 | tf_op jit(solution)/shard_map/ppermute | solution.py:18
  36.6 4.5 %collective-permute-start.10 = (bf16[2,256,512]{2,1,0:T(8,128)(2,1)S(1)}, bf16[2,256,512]{2,1,0:T(8,128)(2,1)S(1)}, u32[]{:S(2)}, u32[]{:S(2)}) collective-permute-start(bf16[2,256,512]{2,1,0:T(8,128)(2,1)S(1)} %collective-permute-done.4.refs_13_), channel_id=1, source_target_pairs={{0,1},{1,0},{2,3},{3,2},{4,5},{5,4},{6,7},{7,6},{8,9},{9,8},{10,11... | collective-permute-start | bytes 1572872 | tf_op jit(solution)/shard_map/ppermute | solution.py:18
  36.7 3.4 %collective-permute-start.6 = (bf16[1296,128]{1,0:T(8,128)(2,1)S(1)}, bf16[1296,128]{1,0:T(8,128)(2,1)S(1)}, u32[]{:S(2)}, u32[]{:S(2)}) collective-permute-start(bf16[1296,128]{1,0:T(8,128)(2,1)S(1)} %collective-permute-done.refs_4_), channel_id=1, source_target_pairs={{0,1},{1,0},{2,3},{3,2},{4,5},{5,4},{6,7},{7,6},{8,9},{9,8},{10,11... | collective-permute-start | bytes 995336 | tf_op jit(solution)/shard_map/ppermute | solution.py:18
  37.1 3.5 %collective-permute-start.7 = (bf16[1296,128]{1,0:T(8,128)(2,1)S(1)}, bf16[1296,128]{1,0:T(8,128)(2,1)S(1)}, u32[]{:S(2)}, u32[]{:S(2)}) collective-permute-start(bf16[1296,128]{1,0:T(8,128)(2,1)S(1)} %collective-permute-done.1.refs_6_), channel_id=1, source_target_pairs={{0,1},{1,0},{2,3},{3,2},{4,5},{5,4},{6,7},{7,6},{8,9},{9,8},{10,11... | collective-permute-start | bytes 995336 | tf_op jit(solution)/shard_map/ppermute | solution.py:18
  37.2 3.9 %collective-permute-start.8 = (bf16[1296,128]{1,0:T(8,128)(2,1)S(1)}, bf16[1296,128]{1,0:T(8,128)(2,1)S(1)}, u32[]{:S(2)}, u32[]{:S(2)}) collective-permute-start(bf16[1296,128]{1,0:T(8,128)(2,1)S(1)} %collective-permute-done.2.refs_8_), channel_id=1, source_target_pairs={{0,1},{1,0},{2,3},{3,2},{4,5},{5,4},{6,7},{7,6},{8,9},{9,8},{10,11... | collective-permute-start | bytes 995336 | tf_op jit(solution)/shard_map/ppermute | solution.py:18
  68.5 8.1 %collective-permute-start.11 = (bf16[256,512]{1,0:T(8,128)(2,1)S(1)}, bf16[256,512]{1,0:T(8,128)(2,1)S(1)}, u32[]{:S(2)}, u32[]{:S(2)}) collective-permute-start(bf16[256,512]{1,0:T(8,128)(2,1)S(1)} %get-tuple-element.24), channel_id=1, source_target_pairs={{0,8},{8,0},{16,24},{24,16},{1,9},{9,1},{17,25},{25,17},{2,10},{10... | collective-permute-start | bytes 786440 | tf_op jit(solution)/shard_map/ppermute | solution.py:18

commit v3 on v2

--- a/solution.py
+++ b/solution.py
@@ -74,8 +74,6 @@
         initial[position] = value
         even[pl.ds(pl.multiple_of((position + 1) * rows, rows), rows)] = value
     to_scalars.wait()
-
-    order = {slot: index for index, slot in enumerate(slots)}
 
     def note(slot, index):
         if in_order:
@@ -219,18 +217,18 @@
     far = [swapped(payload, "dom", mask) for mask in masks]
     up = one_way(layer_weights, ("section", "dom"), route)
     pair = swapped(my_share, "section", 1)
-    mate = swapped(payload, "dom", 1)
-    far, up, pair, mate = lax.optimization_barrier((far, up, pair, mate))
+    far = lax.optimization_barrier(far)
     if in_order:
         parts, own = 2 * layers + 1, jnp.int32(layers)
         slots = tuple(range(parts))
         pieces = [payload if d == 0 else shifted(payload, "dom", d) for d in range(-layers, layers + 1)]
     else:
         parts, own = doms, me
-        slots, pieces = [0, 1], [payload, mate]
+        slots, pieces = [0, 1], [payload, swapped(payload, "dom", 1)]
         for mask, piece in zip(masks, far):
             slots += [mask, mask + 1]
             pieces += [piece, swapped(piece, "dom", 1)]
+        pair, _ = lax.optimization_barrier((pair, pieces[3::2]))
         slots = tuple(slots)
     inputs = [layer_weights, up, swapped(up, "dom", 1), pair, swapped(pair, "dom", 1)]
     shares = [("own", None), ("up", 0), ("up", 1), ("pair", 0), ("pair", 1)]

time: 77.6 us -> 76.5 us (0.986)
  waiting for transfers between devices: 37.2 us -> 28 us
  starting transfers between devices: 9.37 us -> 16.7 us
    ppermute x11, waiting for transfers between devices: 37.2 us -> 12.5 us  [swapped(): lax.ppermute(block, axis, [(i, i ^ mask) for i in range(lax.axis_size(axi...]
    ppermute x1, waiting for transfers between devices: 0.01 us -> 15.5 us  [one_way(): return lax.ppermute(block, axis, pairs)]
    ppermute x11, starting transfers between devices: 8.08 us -> 15.4 us  [swapped(): lax.ppermute(block, axis, [(i, i ^ mask) for i in range(lax.axis_size(axi...]
where the time goes in v3:
time: 76.5 us; the launch traced here: 76.1 us
  waiting for transfers between devices  28 us (37%)
  Pallas kernels  28 us (37%)
  starting transfers between devices  16.7 us (22%)
  local copies, waits for them, and re-layouts  1.71 us (2%)
  other arithmetic  1.66 us (2%)
    pallas_call x1, Pallas kernels, shards(): pl.pallas_call(functools.partial(cone_kernel, dims), out_shape=(jax.Shape...  28 us
    ppermute x1, waiting for transfers between devices, one_way(): return lax.ppermute(block, axis, pairs)  15.5 us
    ppermute x11, starting transfers between devices, swapped(): lax.ppermute(block, axis, [(i, i ^ mask) for i in range(lax.axis_size(axi...  15.4 us
    ppermute x11, waiting for transfers between devices, swapped(): lax.ppermute(block, axis, [(i, i ^ mask) for i in range(lax.axis_size(axi...  12.5 us
  transfers between devices with their start and end apart: 12, of which 6 were waited for; matrix products, arithmetic and copies ran while one was open for 0% of the time, Pallas kernels for 0%

profile of v3, /device:TPU:13, one launch (start us, length us, event | category | flops | bytes accessed | tf_op | source)
XLA Modules:
  0.0 76.1 jit_solution(16147973271919432899)
XLA Ops:
  0.0 0.8 %fusion.7 = bf16[1,2]{1,0:T(2,128)(2,1)S(1)} fusion(s32[2,2]{1,0:T(2,128)} %param.10, s32[]{:T(128)S(6)} %select_n.29), kind=kLoop, calls=%fused_computation.16 | loop fusion | flops 2 | bytes 16 | tf_op jit(solution)/shard_map/convert
  0.8 0.7 fusion.6
  1.5 0.1 concatenate.16
  1.6 0.8 %dynamic-slice_bitcast_fusion = bf16[256,128]{1,0:T(8,128)(2,1)S(1)} fusion(bf16[2,256,128]{2,1,0:T(8,128)(2,1)} %param.6, s32[]{:T(128)S(6)} %select_n.29), kind=kLoop, calls=%fused_computation.2 | loop fusion | bytes 131076 | tf_op jit(solution)/shard_map/jit(dynamic_index_in_dim)/squeeze | solution.py:202
  2.4 0.1 fusion.5
  2.6 1.3 %collective-permute-start.7 = (bf16[2,512,512]{2,1,0:T(8,128)(2,1)S(1)}, bf16[2,512,512]{2,1,0:T(8,128)(2,1)S(1)}, u32[]{:S(2)}, u32[]{:S(2)}) collective-permute-start(bf16[2,512,512]{2,1,0:T(8,128)(2,1)S(1)} %copy-done.1), channel_id=1, source_target_pairs={{0,16},{1,25},{2,18},{3,27},{4,20},{5,29},{6,22},{7,31},{8,24},{9,... | collective-permute-start | bytes 3145736 | tf_op jit(solution)/shard_map/ppermute | solution.py:27
  3.9 1.4 %collective-permute-start.3 = (bf16[1296,128]{1,0:T(8,128)(2,1)S(1)}, bf16[1296,128]{1,0:T(8,128)(2,1)S(1)}, u32[]{:S(2)}, u32[]{:S(2)}) collective-permute-start(bf16[1296,128]{1,0:T(8,128)(2,1)S(1)} %pad_maximum_fusion.refs_2_), channel_id=1, source_target_pairs={{0,6},{1,7},{2,4},{3,5},{4,2},{5,3},{6,0},{7,1},{8,14},{9,15},{10,... | collective-permute-start | bytes 995336 | tf_op jit(solution)/shard_map/ppermute | solution.py:18
  5.2 1.1 %collective-permute-start.2 = (bf16[1296,128]{1,0:T(8,128)(2,1)S(1)}, bf16[1296,128]{1,0:T(8,128)(2,1)}, u32[]{:S(2)}, u32[]{:S(2)}) collective-permute-start(bf16[1296,128]{1,0:T(8,128)(2,1)S(1)} %pad_maximum_fusion.refs_2_), channel_id=1, source_target_pairs={{0,4},{1,5},{2,6},{3,7},{4,0},{5,1},{6,2},{7,3},{8,12},{9,13},{10,... | collective-permute-start | bytes 995336 | tf_op jit(solution)/shard_map/ppermute | solution.py:18
  6.3 1.1 %collective-permute-start.1 = (bf16[1296,128]{1,0:T(8,128)(2,1)S(1)}, bf16[1296,128]{1,0:T(8,128)(2,1)}, u32[]{:S(2)}, u32[]{:S(2)}) collective-permute-start(bf16[1296,128]{1,0:T(8,128)(2,1)S(1)} %pad_maximum_fusion.refs_2_), channel_id=1, source_target_pairs={{0,2},{1,3},{2,0},{3,1},{4,6},{5,7},{6,4},{7,5},{8,10},{9,11},{10,... | collective-permute-start | bytes 995336 | tf_op jit(solution)/shard_map/ppermute | solution.py:18
  7.5 1.3 %collective-permute-start.9 = (bf16[2,256,512]{2,1,0:T(8,128)(2,1)S(1)}, bf16[2,256,512]{2,1,0:T(8,128)(2,1)S(1)}, u32[]{:S(2)}, u32[]{:S(2)}) collective-permute-start(bf16[2,256,512]{2,1,0:T(8,128)(2,1)S(1)} %constant_dynamic-slice_fusion), channel_id=1, source_target_pairs={{0,8},{8,0},{16,24},{24,16},{1,9},{9,1},{17,25},{25,17},{2,10},{10... | collective-permute-start | bytes 1572872 | tf_op jit(solution)/shard_map/ppermute | solution.py:18
  8.7 15.5 %collective-permute-done.7.refs_11_ = bf16[2,512,512]{2,1,0:T(8,128)(2,1)S(1)} collective-permute-done((bf16[2,512,512]{2,1,0:T(8,128)(2,1)S(1)}, bf16[2,512,512]{2,1,0:T(8,128)(2,1)S(1)}, u32[]{:S(2)}, u32[]{:S(2)}) %collective-permute-start.7) | collective-permute-done | bytes 1048608 | tf_op jit(solution)/shard_map/ppermute | solution.py:27
  24.2 6.7 %collective-permute-start.8 = (bf16[2,512,512]{2,1,0:T(8,128)(2,1)S(1)}, bf16[2,512,512]{2,1,0:T(8,128)(2,1)S(1)}, u32[]{:S(2)}, u32[]{:S(2)}) collective-permute-start(bf16[2,512,512]{2,1,0:T(8,128)(2,1)S(1)} %collective-permute-done.7.refs_11_), channel_id=1, source_target_pairs={{0,1},{1,0},{2,3},{3,2},{4,5},{5,4},{6,7},{7,6},{8,9},{9,8},{10,11... | collective-permute-start | bytes 3145736 | tf_op jit(solution)/shard_map/ppermute | solution.py:18
  30.9 0.0 collective-permute-done.3.refs_8_
  30.9 2.1 %collective-permute-done.2.refs_6_ = bf16[1296,128]{1,0:T(8,128)(2,1)} collective-permute-done((bf16[1296,128]{1,0:T(8,128)(2,1)S(1)}, bf16[1296,128]{1,0:T(8,128)(2,1)}, u32[]{:S(2)}, u32[]{:S(2)}) %collective-permute-start.2) | collective-permute-done | bytes 331808 | tf_op jit(solution)/shard_map/ppermute | solution.py:18
  33.0 0.0 collective-permute-done.1.refs_4_
  33.0 1.5 %collective-permute-start.4 = (bf16[1296,128]{1,0:T(8,128)(2,1)}, bf16[1296,128]{1,0:T(8,128)(2,1)S(1)}, u32[]{:S(2)}, u32[]{:S(2)}) collective-permute-start(bf16[1296,128]{1,0:T(8,128)(2,1)} %collective-permute-done.1.refs_4_), channel_id=1, source_target_pairs={{0,1},{1,0},{2,3},{3,2},{4,5},{5,4},{6,7},{7,6},{8,9},{9,8},{10,11... | collective-permute-start | bytes 995336 | tf_op jit(solution)/shard_map/ppermute | solution.py:18
  34.6 0.0 collective-permute-start.5
  34.6 0.5 collective-permute-start.6
  35.1 0.0 collective-permute-done.9.refs_13_
  35.1 1.0 %collective-permute-done.4.refs_5_ = bf16[1296,128]{1,0:T(8,128)(2,1)S(1)} collective-permute-done((bf16[1296,128]{1,0:T(8,128)(2,1)}, bf16[1296,128]{1,0:T(8,128)(2,1)S(1)}, u32[]{:S(2)}, u32[]{:S(2)}) %collective-permute-start.4) | collective-permute-done | bytes 331808 | tf_op jit(solution)/shard_map/ppermute | solution.py:18
  36.0 0.8 %collective-permute-done.5.refs_7_ = bf16[1296,128]{1,0:T(8,128)(2,1)S(1)} collective-permute-done((bf16[1296,128]{1,0:T(8,128)(2,1)}, bf16[1296,128]{1,0:T(8,128)(2,1)S(1)}, u32[]{:S(2)}, u32[]{:S(2)}) %collective-permute-start.5) | collective-permute-done | bytes 331808 | tf_op jit(solution)/shard_map/ppermute | solution.py:18
  36.9 0.0 collective-permute-done.6.refs_9_
  36.9 0.3 collective-permute-start.10
  37.2 0.2 collective-permute-start
  37.4 0.1 pad_add_fusion.refs_0_
  37.4 1.8 %collective-permute-done.refs_3_ = bf16[1296,128]{1,0:T(8,128)(2,1)S(1)} collective-permute-done((bf16[1296,128]{1,0:T(8,128)(2,1)S(1)}, bf16[1296,128]{1,0:T(8,128)(2,1)S(1)}, u32[]{:S(2)}, u32[]{:S(2)}) %collective-permute-start) | collective-permute-done | bytes 331808 | tf_op jit(solution)/shard_map/ppermute | solution.py:18
  39.2 0.0 collective-permute-done.10.refs_14_
  39.2 0.0 collective-permute-done.8.refs_12_
  39.3 28.0 %shard_map.64 = (bf16[1,2,256,512]{3,2,1,0:T(8,128)(2,1)}, bf16[256,512]{1,0:T(8,128)(2,1)S(1)}) custom-call(s32[4]{0:T(128)S(1)} %pad_add_fusion.refs_0_, bf16[128,512]{1,0:T(8,128)(2,1)S(1)} %copy-done.2, bf16[1296,128]{1,0:T(8,128)(2,1)S(1)} %pad_maximum_fusion.refs_2_, bf16[1296,128]{1,0:T(8,128)(2,1)S(1)} %collective-permute-done.refs_3_, ...), custom_call_target="tpu_custom_call" | custom-call | tf_op jit(solution)/shard_map/pallas_call | solution.py:243
  67.2 1.3 %collective-permute-start.11 = (bf16[256,512]{1,0:T(8,128)(2,1)S(1)}, bf16[256,512]{1,0:T(8,128)(2,1)S(1)}, u32[]{:S(2)}, u32[]{:S(2)}) collective-permute-start(bf16[256,512]{1,0:T(8,128)(2,1)S(1)} %get-tuple-element.20), channel_id=1, source_target_pairs={{0,8},{8,0},{16,24},{24,16},{1,9},{9,1},{17,25},{25,17},{2,10},{10... | collective-permute-start | bytes 786440 | tf_op jit(solution)/shard_map/ppermute | solution.py:18
  68.6 6.8 %collective-permute-done.11 = bf16[256,512]{1,0:T(8,128)(2,1)S(1)} collective-permute-done((bf16[256,512]{1,0:T(8,128)(2,1)S(1)}, bf16[256,512]{1,0:T(8,128)(2,1)S(1)}, u32[]{:S(2)}, u32[]{:S(2)}) %collective-permute-start.11) | collective-permute-done | bytes 262176 | tf_op jit(solution)/shard_map/ppermute | solution.py:18
  75.4 0.7 bitcast_dynamic-update-slice_fusion
  (9 shorter events, 0.1 us)
Async XLA Ops:
  0.0 2.4 %copy-start = (bf16[2,2,4,128,128]{4,3,2,1,0:T(8,128)(2,1)S(1)}, bf16[2,2,4,128,128]{4,3,2,1,0:T(8,128)(2,1)}, u32[]{:S(2)}) copy-start(bf16[2,2,4,128,128]{4,3,2,1,0:T(8,128)(2,1)} %param.9) | copy-start | bytes 1572868
  0.0 2.6 %copy-start.1 = (bf16[2,512,512]{2,1,0:T(8,128)(2,1)S(1)}, bf16[2,512,512]{2,1,0:T(8,128)(2,1)}, u32[]{:S(2)}) copy-start(bf16[2,512,512]{2,1,0:T(8,128)(2,1)} %refs_10_) | copy-start | bytes 3145732
  2.6 21.7 %collective-permute-start.7 = (bf16[2,512,512]{2,1,0:T(8,128)(2,1)S(1)}, bf16[2,512,512]{2,1,0:T(8,128)(2,1)S(1)}, u32[]{:S(2)}, u32[]{:S(2)}) collective-permute-start(bf16[2,512,512]{2,1,0:T(8,128)(2,1)S(1)} %copy-done.1), channel_id=1, source_target_pairs={{0,16},{1,25},{2,18},{3,27},{4,20},{5,29},{6,22},{7,31},{8,24},{9,... | collective-permute-start | bytes 3145736 | tf_op jit(solution)/shard_map/ppermute | solution.py:27
  3.9 27.1 %collective-permute-start.3 = (bf16[1296,128]{1,0:T(8,128)(2,1)S(1)}, bf16[1296,128]{1,0:T(8,128)(2,1)S(1)}, u32[]{:S(2)}, u32[]{:S(2)}) collective-permute-start(bf16[1296,128]{1,0:T(8,128)(2,1)S(1)} %pad_maximum_fusion.refs_2_), channel_id=1, source_target_pairs={{0,6},{1,7},{2,4},{3,5},{4,2},{5,3},{6,0},{7,1},{8,14},{9,15},{10,... | collective-permute-start | bytes 995336 | tf_op jit(solution)/shard_map/ppermute | solution.py:18
  5.2 27.8 %collective-permute-start.2 = (bf16[1296,128]{1,0:T(8,128)(2,1)S(1)}, bf16[1296,128]{1,0:T(8,128)(2,1)}, u32[]{:S(2)}, u32[]{:S(2)}) collective-permute-start(bf16[1296,128]{1,0:T(8,128)(2,1)S(1)} %pad_maximum_fusion.refs_2_), channel_id=1, source_target_pairs={{0,4},{1,5},{2,6},{3,7},{4,0},{5,1},{6,2},{7,3},{8,12},{9,13},{10,... | collective-permute-start | bytes 995336 | tf_op jit(solution)/shard_map/ppermute | solution.py:18
  6.3 26.7 %collective-permute-start.1 = (bf16[1296,128]{1,0:T(8,128)(2,1)S(1)}, bf16[1296,128]{1,0:T(8,128)(2,1)}, u32[]{:S(2)}, u32[]{:S(2)}) collective-permute-start(bf16[1296,128]{1,0:T(8,128)(2,1)S(1)} %pad_maximum_fusion.refs_2_), channel_id=1, source_target_pairs={{0,2},{1,3},{2,0},{3,1},{4,6},{5,7},{6,4},{7,5},{8,10},{9,11},{10,... | collective-permute-start | bytes 995336 | tf_op jit(solution)/shard_map/ppermute | solution.py:18
  7.4 31.8 %copy-start.2 = (bf16[128,512]{1,0:T(8,128)(2,1)S(1)}, bf16[128,512]{1,0:T(8,128)(2,1)}, u32[]{:S(2)}) copy-start(bf16[128,512]{1,0:T(8,128)(2,1)} %refs_1_.1) | copy-start | bytes 393220
  7.5 27.6 %collective-permute-start.9 = (bf16[2,256,512]{2,1,0:T(8,128)(2,1)S(1)}, bf16[2,256,512]{2,1,0:T(8,128)(2,1)S(1)}, u32[]{:S(2)}, u32[]{:S(2)}) collective-permute-start(bf16[2,256,512]{2,1,0:T(8,128)(2,1)S(1)} %constant_dynamic-slice_fusion), channel_id=1, source_target_pairs={{0,8},{8,0},{16,24},{24,16},{1,9},{9,1},{17,25},{25,17},{2,10},{10... | collective-permute-start | bytes 1572872 | tf_op jit(solution)/shard_map/ppermute | solution.py:18
  24.2 15.0 %collective-permute-start.8 = (bf16[2,512,512]{2,1,0:T(8,128)(2,1)S(1)}, bf16[2,512,512]{2,1,0:T(8,128)(2,1)S(1)}, u32[]{:S(2)}, u32[]{:S(2)}) collective-permute-start(bf16[2,512,512]{2,1,0:T(8,128)(2,1)S(1)} %collective-permute-done.7.refs_11_), channel_id=1, source_target_pairs={{0,1},{1,0},{2,3},{3,2},{4,5},{5,4},{6,7},{7,6},{8,9},{9,8},{10,11... | collective-permute-start | bytes 3145736 | tf_op jit(solution)/shard_map/ppermute | solution.py:18
  33.0 3.0 %collective-permute-start.4 = (bf16[1296,128]{1,0:T(8,128)(2,1)}, bf16[1296,128]{1,0:T(8,128)(2,1)S(1)}, u32[]{:S(2)}, u32[]{:S(2)}) collective-permute-start(bf16[1296,128]{1,0:T(8,128)(2,1)} %collective-permute-done.1.refs_4_), channel_id=1, source_target_pairs={{0,1},{1,0},{2,3},{3,2},{4,5},{5,4},{6,7},{7,6},{8,9},{9,8},{10,11... | collective-permute-start | bytes 995336 | tf_op jit(solution)/shard_map/ppermute | solution.py:18
  34.6 2.3 %collective-permute-start.5 = (bf16[1296,128]{1,0:T(8,128)(2,1)}, bf16[1296,128]{1,0:T(8,128)(2,1)S(1)}, u32[]{:S(2)}, u32[]{:S(2)}) collective-permute-start(bf16[1296,128]{1,0:T(8,128)(2,1)} %collective-permute-done.2.refs_6_), channel_id=1, source_target_pairs={{0,1},{1,0},{2,3},{3,2},{4,5},{5,4},{6,7},{7,6},{8,9},{9,8},{10,11... | collective-permute-start | bytes 995336 | tf_op jit(solution)/shard_map/ppermute | solution.py:18
  34.6 2.3 %collective-permute-start.6 = (bf16[1296,128]{1,0:T(8,128)(2,1)S(1)}, bf16[1296,128]{1,0:T(8,128)(2,1)S(1)}, u32[]{:S(2)}, u32[]{:S(2)}) collective-permute-start(bf16[1296,128]{1,0:T(8,128)(2,1)S(1)} %collective-permute-done.3.refs_8_), channel_id=1, source_target_pairs={{0,1},{1,0},{2,3},{3,2},{4,5},{5,4},{6,7},{7,6},{8,9},{9,8},{10,11... | collective-permute-start | bytes 995336 | tf_op jit(solution)/shard_map/ppermute | solution.py:18
  36.9 2.4 %collective-permute-start.10 = (bf16[2,256,512]{2,1,0:T(8,128)(2,1)S(1)}, bf16[2,256,512]{2,1,0:T(8,128)(2,1)S(1)}, u32[]{:S(2)}, u32[]{:S(2)}) collective-permute-start(bf16[2,256,512]{2,1,0:T(8,128)(2,1)S(1)} %collective-permute-done.9.refs_13_), channel_id=1, source_target_pairs={{0,1},{1,0},{2,3},{3,2},{4,5},{5,4},{6,7},{7,6},{8,9},{9,8},{10,11... | collective-permute-start | bytes 1572872 | tf_op jit(solution)/shard_map/ppermute | solution.py:18
  37.2 2.1 %collective-permute-start = (bf16[1296,128]{1,0:T(8,128)(2,1)S(1)}, bf16[1296,128]{1,0:T(8,128)(2,1)S(1)}, u32[]{:S(2)}, u32[]{:S(2)}) collective-permute-start(bf16[1296,128]{1,0:T(8,128)(2,1)S(1)} %pad_maximum_fusion.refs_2_), channel_id=1, source_target_pairs={{0,1},{1,0},{2,3},{3,2},{4,5},{5,4},{6,7},{7,6},{8,9},{9,8},{10,11... | collective-permute-start | bytes 995336 | tf_op jit(solution)/shard_map/ppermute | solution.py:18
  67.2 8.2 %collective-permute-start.11 = (bf16[256,512]{1,0:T(8,128)(2,1)S(1)}, bf16[256,512]{1,0:T(8,128)(2,1)S(1)}, u32[]{:S(2)}, u32[]{:S(2)}) collective-permute-start(bf16[256,512]{1,0:T(8,128)(2,1)S(1)} %get-tuple-element.20), channel_id=1, source_target_pairs={{0,8},{8,0},{16,24},{24,16},{1,9},{9,1},{17,25},{25,17},{2,10},{10... | collective-permute-start | bytes 786440 | tf_op jit(solution)/shard_map/ppermute | solution.py:18

commit v4 on v2

--- a/solution.py
+++ b/solution.py
@@ -74,8 +74,6 @@
         initial[position] = value
         even[pl.ds(pl.multiple_of((position + 1) * rows, rows), rows)] = value
     to_scalars.wait()
-
-    order = {slot: index for index, slot in enumerate(slots)}
 
     def note(slot, index):
         if in_order:
@@ -220,7 +218,7 @@
     up = one_way(layer_weights, ("section", "dom"), route)
     pair = swapped(my_share, "section", 1)
     mate = swapped(payload, "dom", 1)
-    far, up, pair, mate = lax.optimization_barrier((far, up, pair, mate))
+    far, mate = lax.optimization_barrier((far, mate))
     if in_order:
         parts, own = 2 * layers + 1, jnp.int32(layers)
         slots = tuple(range(parts))
@@ -231,6 +229,7 @@
         for mask, piece in zip(masks, far):
             slots += [mask, mask + 1]
             pieces += [piece, swapped(piece, "dom", 1)]
+        pair, _ = lax.optimization_barrier((pair, pieces[3::2]))
         slots = tuple(slots)
     inputs = [layer_weights, up, swapped(up, "dom", 1), pair, swapped(pair, "dom", 1)]
     shares = [("own", None), ("up", 0), ("up", 1), ("pair", 0), ("pair", 1)]

time: 77.6 us -> 76.7 us (0.988)
  waiting for transfers between devices: 37.2 us -> 28 us
  starting transfers between devices: 9.37 us -> 17 us
    ppermute x11, waiting for transfers between devices: 37.2 us -> 13.7 us  [swapped(): lax.ppermute(block, axis, [(i, i ^ mask) for i in range(lax.axis_size(axi...]
    ppermute x1, waiting for transfers between devices: 0.01 us -> 14.3 us  [one_way(): return lax.ppermute(block, axis, pairs)]
    ppermute x11, starting transfers between devices: 8.08 us -> 15.7 us  [swapped(): lax.ppermute(block, axis, [(i, i ^ mask) for i in range(lax.axis_size(axi...]
  transfers between devices with their start and end apart: 12 -> 12, of which waited for: 6 -> 7; matrix products, arithmetic and copies ran while one was open for 0% -> 0% of each run, Pallas kernels for 0% -> 0%
where the time goes in v4:
time: 76.7 us; the launch traced here: 76.5 us
  waiting for transfers between devices  28 us (37%)
  Pallas kernels  28 us (37%)
  starting transfers between devices  17 us (22%)
  local copies, waits for them, and re-layouts  1.71 us (2%)
  other arithmetic  1.66 us (2%)
    pallas_call x1, Pallas kernels, shards(): pl.pallas_call(functools.partial(cone_kernel, dims), out_shape=(jax.Shape...  28 us
    ppermute x11, starting transfers between devices, swapped(): lax.ppermute(block, axis, [(i, i ^ mask) for i in range(lax.axis_size(axi...  15.7 us
    ppermute x1, waiting for transfers between devices, one_way(): return lax.ppermute(block, axis, pairs)  14.3 us
    ppermute x11, waiting for transfers between devices, swapped(): lax.ppermute(block, axis, [(i, i ^ mask) for i in range(lax.axis_size(axi...  13.7 us
  transfers between devices with their start and end apart: 12, of which 7 were waited for; matrix products, arithmetic and copies ran while one was open for 0% of the time, Pallas kernels for 0%

profile of v4, /device:TPU:13, one launch (start us, length us, event | category | flops | bytes accessed | tf_op | source)
XLA Modules:
  0.0 76.5 jit_solution(5284091168859731750)
XLA Ops:
  0.0 0.8 %fusion.7 = bf16[1,2]{1,0:T(2,128)(2,1)S(1)} fusion(s32[2,2]{1,0:T(2,128)} %param.10, s32[]{:T(128)S(6)} %select_n.29), kind=kLoop, calls=%fused_computation.16 | loop fusion | flops 2 | bytes 16 | tf_op jit(solution)/shard_map/convert
  0.8 0.7 fusion.6
  1.5 0.1 concatenate.16
  1.6 0.8 %dynamic-slice_bitcast_fusion = bf16[256,128]{1,0:T(8,128)(2,1)S(1)} fusion(bf16[2,256,128]{2,1,0:T(8,128)(2,1)} %param.6, s32[]{:T(128)S(6)} %select_n.29), kind=kLoop, calls=%fused_computation.2 | loop fusion | bytes 131076 | tf_op jit(solution)/shard_map/jit(dynamic_index_in_dim)/squeeze | solution.py:202
  2.4 0.1 fusion.5
  2.6 1.3 %collective-permute-start.7 = (bf16[2,512,512]{2,1,0:T(8,128)(2,1)S(1)}, bf16[2,512,512]{2,1,0:T(8,128)(2,1)S(1)}, u32[]{:S(2)}, u32[]{:S(2)}) collective-permute-start(bf16[2,512,512]{2,1,0:T(8,128)(2,1)S(1)} %copy-done.1), channel_id=1, source_target_pairs={{0,16},{1,25},{2,18},{3,27},{4,20},{5,29},{6,22},{7,31},{8,24},{9,... | collective-permute-start | bytes 3145736 | tf_op jit(solution)/shard_map/ppermute | solution.py:27
  3.9 0.7 collective-permute-start.3
  4.6 1.3 %collective-permute-start.2 = (bf16[1296,128]{1,0:T(8,128)(2,1)S(1)}, bf16[1296,128]{1,0:T(8,128)(2,1)}, u32[]{:S(2)}, u32[]{:S(2)}) collective-permute-start(bf16[1296,128]{1,0:T(8,128)(2,1)S(1)} %pad_maximum_fusion.refs_2_), channel_id=1, source_target_pairs={{0,6},{1,7},{2,4},{3,5},{4,2},{5,3},{6,0},{7,1},{8,14},{9,15},{10,... | collective-permute-start | bytes 995336 | tf_op jit(solution)/shard_map/ppermute | solution.py:18
  5.9 1.0 %collective-permute-start.1 = (bf16[1296,128]{1,0:T(8,128)(2,1)S(1)}, bf16[1296,128]{1,0:T(8,128)(2,1)}, u32[]{:S(2)}, u32[]{:S(2)}) collective-permute-start(bf16[1296,128]{1,0:T(8,128)(2,1)S(1)} %pad_maximum_fusion.refs_2_), channel_id=1, source_target_pairs={{0,4},{1,5},{2,6},{3,7},{4,0},{5,1},{6,2},{7,3},{8,12},{9,13},{10,... | collective-permute-start | bytes 995336 | tf_op jit(solution)/shard_map/ppermute | solution.py:18
  6.9 1.2 %collective-permute-start = (bf16[1296,128]{1,0:T(8,128)(2,1)S(1)}, bf16[1296,128]{1,0:T(8,128)(2,1)}, u32[]{:S(2)}, u32[]{:S(2)}) collective-permute-start(bf16[1296,128]{1,0:T(8,128)(2,1)S(1)} %pad_maximum_fusion.refs_2_), channel_id=1, source_target_pairs={{0,2},{1,3},{2,0},{3,1},{4,6},{5,7},{6,4},{7,5},{8,10},{9,11},{10,... | collective-permute-start | bytes 995336 | tf_op jit(solution)/shard_map/ppermute | solution.py:18
  8.2 0.0 collective-permute-done.3.refs_3_
  8.2 1.3 %collective-permute-start.9 = (bf16[2,256,512]{2,1,0:T(8,128)(2,1)S(1)}, bf16[2,256,512]{2,1,0:T(8,128)(2,1)S(1)}, u32[]{:S(2)}, u32[]{:S(2)}) collective-permute-start(bf16[2,256,512]{2,1,0:T(8,128)(2,1)S(1)} %constant_dynamic-slice_fusion), channel_id=1, source_target_pairs={{0,8},{8,0},{16,24},{24,16},{1,9},{9,1},{17,25},{25,17},{2,10},{10... | collective-permute-start | bytes 1572872 | tf_op jit(solution)/shard_map/ppermute | solution.py:18
  9.4 14.3 %collective-permute-done.7.refs_11_ = bf16[2,512,512]{2,1,0:T(8,128)(2,1)S(1)} collective-permute-done((bf16[2,512,512]{2,1,0:T(8,128)(2,1)S(1)}, bf16[2,512,512]{2,1,0:T(8,128)(2,1)S(1)}, u32[]{:S(2)}, u32[]{:S(2)}) %collective-permute-start.7) | collective-permute-done | bytes 1048608 | tf_op jit(solution)/shard_map/ppermute | solution.py:27
  23.8 7.2 %collective-permute-start.8 = (bf16[2,512,512]{2,1,0:T(8,128)(2,1)S(1)}, bf16[2,512,512]{2,1,0:T(8,128)(2,1)S(1)}, u32[]{:S(2)}, u32[]{:S(2)}) collective-permute-start(bf16[2,512,512]{2,1,0:T(8,128)(2,1)S(1)} %collective-permute-done.7.refs_11_), channel_id=1, source_target_pairs={{0,1},{1,0},{2,3},{3,2},{4,5},{5,4},{6,7},{7,6},{8,9},{9,8},{10,11... | collective-permute-start | bytes 3145736 | tf_op jit(solution)/shard_map/ppermute | solution.py:18
  30.9 0.0 collective-permute-done.2.refs_8_
  30.9 3.5 %collective-permute-done.1.refs_6_ = bf16[1296,128]{1,0:T(8,128)(2,1)} collective-permute-done((bf16[1296,128]{1,0:T(8,128)(2,1)S(1)}, bf16[1296,128]{1,0:T(8,128)(2,1)}, u32[]{:S(2)}, u32[]{:S(2)}) %collective-permute-start.1) | collective-permute-done | bytes 331808 | tf_op jit(solution)/shard_map/ppermute | solution.py:18
  34.4 0.0 collective-permute-done.refs_4_
  34.4 0.8 %collective-permute-start.4 = (bf16[1296,128]{1,0:T(8,128)(2,1)}, bf16[1296,128]{1,0:T(8,128)(2,1)S(1)}, u32[]{:S(2)}, u32[]{:S(2)}) collective-permute-start(bf16[1296,128]{1,0:T(8,128)(2,1)} %collective-permute-done.refs_4_), channel_id=1, source_target_pairs={{0,1},{1,0},{2,3},{3,2},{4,5},{5,4},{6,7},{7,6},{8,9},{9,8},{10,11... | collective-permute-start | bytes 995336 | tf_op jit(solution)/shard_map/ppermute | solution.py:18
  35.3 0.0 collective-permute-start.5
  35.3 0.5 collective-permute-start.6
  35.8 0.0 collective-permute-done.9.refs_13_
  35.8 1.0 %collective-permute-done.4.refs_5_ = bf16[1296,128]{1,0:T(8,128)(2,1)S(1)} collective-permute-done((bf16[1296,128]{1,0:T(8,128)(2,1)}, bf16[1296,128]{1,0:T(8,128)(2,1)S(1)}, u32[]{:S(2)}, u32[]{:S(2)}) %collective-permute-start.4) | collective-permute-done | bytes 331808 | tf_op jit(solution)/shard_map/ppermute | solution.py:18
  36.7 0.5 collective-permute-done.5.refs_7_
  37.2 0.5 collective-permute-done.6.refs_9_
  37.7 0.4 collective-permute-start.10
  38.1 0.1 pad_add_fusion.refs_0_
  38.1 1.5 %collective-permute-done.10.refs_14_ = bf16[2,256,512]{2,1,0:T(8,128)(2,1)S(1)} collective-permute-done((bf16[2,256,512]{2,1,0:T(8,128)(2,1)S(1)}, bf16[2,256,512]{2,1,0:T(8,128)(2,1)S(1)}, u32[]{:S(2)}, u32[]{:S(2)}) %collective-permute-start.10) | collective-permute-done | bytes 524320 | tf_op jit(solution)/shard_map/ppermute | solution.py:18
  39.6 0.0 collective-permute-done.8.refs_12_
  39.6 28.0 %shard_map.64 = (bf16[1,2,256,512]{3,2,1,0:T(8,128)(2,1)}, bf16[256,512]{1,0:T(8,128)(2,1)S(1)}) custom-call(s32[4]{0:T(128)S(1)} %pad_add_fusion.refs_0_, bf16[128,512]{1,0:T(8,128)(2,1)S(1)} %copy-done.2, bf16[1296,128]{1,0:T(8,128)(2,1)S(1)} %pad_maximum_fusion.refs_2_, bf16[1296,128]{1,0:T(8,128)(2,1)S(1)} %collective-permute-done.3.refs_3_, ...), custom_call_target="tpu_custom_call" | custom-call | tf_op jit(solution)/shard_map/pallas_call | solution.py:244
  67.6 1.3 %collective-permute-start.11 = (bf16[256,512]{1,0:T(8,128)(2,1)S(1)}, bf16[256,512]{1,0:T(8,128)(2,1)S(1)}, u32[]{:S(2)}, u32[]{:S(2)}) collective-permute-start(bf16[256,512]{1,0:T(8,128)(2,1)S(1)} %get-tuple-element.22), channel_id=1, source_target_pairs={{0,8},{8,0},{16,24},{24,16},{1,9},{9,1},{17,25},{25,17},{2,10},{10... | collective-permute-start | bytes 786440 | tf_op jit(solution)/shard_map/ppermute | solution.py:18
  68.9 6.9 %collective-permute-done.11 = bf16[256,512]{1,0:T(8,128)(2,1)S(1)} collective-permute-done((bf16[256,512]{1,0:T(8,128)(2,1)S(1)}, bf16[256,512]{1,0:T(8,128)(2,1)S(1)}, u32[]{:S(2)}, u32[]{:S(2)}) %collective-permute-start.11) | collective-permute-done | bytes 262176 | tf_op jit(solution)/shard_map/ppermute | solution.py:18
  75.8 0.7 bitcast_dynamic-update-slice_fusion
  (9 shorter events, 0.1 us)
Async XLA Ops:
  0.0 2.4 %copy-start = (bf16[2,2,4,128,128]{4,3,2,1,0:T(8,128)(2,1)S(1)}, bf16[2,2,4,128,128]{4,3,2,1,0:T(8,128)(2,1)}, u32[]{:S(2)}) copy-start(bf16[2,2,4,128,128]{4,3,2,1,0:T(8,128)(2,1)} %param.9) | copy-start | bytes 1572868
  0.0 2.6 %copy-start.1 = (bf16[2,512,512]{2,1,0:T(8,128)(2,1)S(1)}, bf16[2,512,512]{2,1,0:T(8,128)(2,1)}, u32[]{:S(2)}) copy-start(bf16[2,512,512]{2,1,0:T(8,128)(2,1)} %refs_10_) | copy-start | bytes 3145732
  2.6 21.2 %collective-permute-start.7 = (bf16[2,512,512]{2,1,0:T(8,128)(2,1)S(1)}, bf16[2,512,512]{2,1,0:T(8,128)(2,1)S(1)}, u32[]{:S(2)}, u32[]{:S(2)}) collective-permute-start(bf16[2,512,512]{2,1,0:T(8,128)(2,1)S(1)} %copy-done.1), channel_id=1, source_target_pairs={{0,16},{1,25},{2,18},{3,27},{4,20},{5,29},{6,22},{7,31},{8,24},{9,... | collective-permute-start | bytes 3145736 | tf_op jit(solution)/shard_map/ppermute | solution.py:27
  3.9 4.3 %collective-permute-start.3 = (bf16[1296,128]{1,0:T(8,128)(2,1)S(1)}, bf16[1296,128]{1,0:T(8,128)(2,1)S(1)}, u32[]{:S(2)}, u32[]{:S(2)}) collective-permute-start(bf16[1296,128]{1,0:T(8,128)(2,1)S(1)} %pad_maximum_fusion.refs_2_), channel_id=1, source_target_pairs={{0,1},{1,0},{2,3},{3,2},{4,5},{5,4},{6,7},{7,6},{8,9},{9,8},{10,11... | collective-permute-start | bytes 995336 | tf_op jit(solution)/shard_map/ppermute | solution.py:18
  4.6 26.3 %collective-permute-start.2 = (bf16[1296,128]{1,0:T(8,128)(2,1)S(1)}, bf16[1296,128]{1,0:T(8,128)(2,1)}, u32[]{:S(2)}, u32[]{:S(2)}) collective-permute-start(bf16[1296,128]{1,0:T(8,128)(2,1)S(1)} %pad_maximum_fusion.refs_2_), channel_id=1, source_target_pairs={{0,6},{1,7},{2,4},{3,5},{4,2},{5,3},{6,0},{7,1},{8,14},{9,15},{10,... | collective-permute-start | bytes 995336 | tf_op jit(solution)/shard_map/ppermute | solution.py:18
  5.9 28.5 %collective-permute-start.1 = (bf16[1296,128]{1,0:T(8,128)(2,1)S(1)}, bf16[1296,128]{1,0:T(8,128)(2,1)}, u32[]{:S(2)}, u32[]{:S(2)}) collective-permute-start(bf16[1296,128]{1,0:T(8,128)(2,1)S(1)} %pad_maximum_fusion.refs_2_), channel_id=1, source_target_pairs={{0,4},{1,5},{2,6},{3,7},{4,0},{5,1},{6,2},{7,3},{8,12},{9,13},{10,... | collective-permute-start | bytes 995336 | tf_op jit(solution)/shard_map/ppermute | solution.py:18
  6.9 27.5 %collective-permute-start = (bf16[1296,128]{1,0:T(8,128)(2,1)S(1)}, bf16[1296,128]{1,0:T(8,128)(2,1)}, u32[]{:S(2)}, u32[]{:S(2)}) collective-permute-start(bf16[1296,128]{1,0:T(8,128)(2,1)S(1)} %pad_maximum_fusion.refs_2_), channel_id=1, source_target_pairs={{0,2},{1,3},{2,0},{3,1},{4,6},{5,7},{6,4},{7,5},{8,10},{9,11},{10,... | collective-permute-start | bytes 995336 | tf_op jit(solution)/shard_map/ppermute | solution.py:18
  8.1 31.5 %copy-start.2 = (bf16[128,512]{1,0:T(8,128)(2,1)S(1)}, bf16[128,512]{1,0:T(8,128)(2,1)}, u32[]{:S(2)}) copy-start(bf16[128,512]{1,0:T(8,128)(2,1)} %refs_1_.1) | copy-start | bytes 393220
  8.2 27.6 %collective-permute-start.9 = (bf16[2,256,512]{2,1,0:T(8,128)(2,1)S(1)}, bf16[2,256,512]{2,1,0:T(8,128)(2,1)S(1)}, u32[]{:S(2)}, u32[]{:S(2)}) collective-permute-start(bf16[2,256,512]{2,1,0:T(8,128)(2,1)S(1)} %constant_dynamic-slice_fusion), channel_id=1, source_target_pairs={{0,8},{8,0},{16,24},{24,16},{1,9},{9,1},{17,25},{25,17},{2,10},{10... | collective-permute-start | bytes 1572872 | tf_op jit(solution)/shard_map/ppermute | solution.py:18
  23.8 15.8 %collective-permute-start.8 = (bf16[2,512,512]{2,1,0:T(8,128)(2,1)S(1)}, bf16[2,512,512]{2,1,0:T(8,128)(2,1)S(1)}, u32[]{:S(2)}, u32[]{:S(2)}) collective-permute-start(bf16[2,512,512]{2,1,0:T(8,128)(2,1)S(1)} %collective-permute-done.7.refs_11_), channel_id=1, source_target_pairs={{0,1},{1,0},{2,3},{3,2},{4,5},{5,4},{6,7},{7,6},{8,9},{9,8},{10,11... | collective-permute-start | bytes 3145736 | tf_op jit(solution)/shard_map/ppermute | solution.py:18
  34.4 2.3 %collective-permute-start.4 = (bf16[1296,128]{1,0:T(8,128)(2,1)}, bf16[1296,128]{1,0:T(8,128)(2,1)S(1)}, u32[]{:S(2)}, u32[]{:S(2)}) collective-permute-start(bf16[1296,128]{1,0:T(8,128)(2,1)} %collective-permute-done.refs_4_), channel_id=1, source_target_pairs={{0,1},{1,0},{2,3},{3,2},{4,5},{5,4},{6,7},{7,6},{8,9},{9,8},{10,11... | collective-permute-start | bytes 995336 | tf_op jit(solution)/shard_map/ppermute | solution.py:18
  35.3 1.9 %collective-permute-start.5 = (bf16[1296,128]{1,0:T(8,128)(2,1)}, bf16[1296,128]{1,0:T(8,128)(2,1)S(1)}, u32[]{:S(2)}, u32[]{:S(2)}) collective-permute-start(bf16[1296,128]{1,0:T(8,128)(2,1)} %collective-permute-done.1.refs_6_), channel_id=1, source_target_pairs={{0,1},{1,0},{2,3},{3,2},{4,5},{5,4},{6,7},{7,6},{8,9},{9,8},{10,11... | collective-permute-start | bytes 995336 | tf_op jit(solution)/shard_map/ppermute | solution.py:18
  35.3 2.4 %collective-permute-start.6 = (bf16[1296,128]{1,0:T(8,128)(2,1)}, bf16[1296,128]{1,0:T(8,128)(2,1)S(1)}, u32[]{:S(2)}, u32[]{:S(2)}) collective-permute-start(bf16[1296,128]{1,0:T(8,128)(2,1)} %collective-permute-done.2.refs_8_), channel_id=1, source_target_pairs={{0,1},{1,0},{2,3},{3,2},{4,5},{5,4},{6,7},{7,6},{8,9},{9,8},{10,11... | collective-permute-start | bytes 995336 | tf_op jit(solution)/shard_map/ppermute | solution.py:18
  37.7 1.9 %collective-permute-start.10 = (bf16[2,256,512]{2,1,0:T(8,128)(2,1)S(1)}, bf16[2,256,512]{2,1,0:T(8,128)(2,1)S(1)}, u32[]{:S(2)}, u32[]{:S(2)}) collective-permute-start(bf16[2,256,512]{2,1,0:T(8,128)(2,1)S(1)} %collective-permute-done.9.refs_13_), channel_id=1, source_target_pairs={{0,1},{1,0},{2,3},{3,2},{4,5},{5,4},{6,7},{7,6},{8,9},{9,8},{10,11... | collective-permute-start | bytes 1572872 | tf_op jit(solution)/shard_map/ppermute | solution.py:18
  67.6 8.2 %collective-permute-start.11 = (bf16[256,512]{1,0:T(8,128)(2,1)S(1)}, bf16[256,512]{1,0:T(8,128)(2,1)S(1)}, u32[]{:S(2)}, u32[]{:S(2)}) collective-permute-start(bf16[256,512]{1,0:T(8,128)(2,1)S(1)} %get-tuple-element.22), channel_id=1, source_target_pairs={{0,8},{8,0},{16,24},{24,16},{1,9},{9,1},{17,25},{25,17},{2,10},{10... | collective-permute-start | bytes 786440 | tf_op jit(solution)/shard_map/ppermute | solution.py:18
